TPU v7x, 32 devices: a whole 2x2x4 slice. The times are simulated.
32 devices in a mesh: dp: 8 (over z, y), tensor: 4 (over x, core).
Axes of the slice: x: 2, y: 2, z: 4, core: 2. Of those that a mesh axis runs over, the one named last changes fastest.
Arguments:
- text_input: bfloat16 [16, 512, 768], P('dp', 'tensor'), may hold values from -6 to 6
- visual_input: bfloat16 [16, 512, 768], P('dp', 'tensor'), may hold values from -6 to 6
- text_boxes: int32 [16, 2, 512], P('dp'), may hold values from 0 to 999
- text_count: int32 [16], P('dp'), may hold values from 20 to 512, as said below
- text_prenorm: bfloat16 [768], replicated, may hold values from 0.5 to 1.5
- text_query: bfloat16 [768, 768], P(None, 'tensor'), may hold values from -0.21875 to 0.21875
- text_key: bfloat16 [768, 768], P(None, 'tensor'), may hold values from -0.21875 to 0.21875
- text_value: bfloat16 [768, 768], P(None, 'tensor'), may hold values from -0.21875 to 0.21875
- text_output: bfloat16 [768, 768], P('tensor'), may hold values from -0.625 to 0.625
- text_midnorm: bfloat16 [768], replicated, may hold values from 0.5 to 1.5
- text_expand: bfloat16 [768, 3072], P(None, 'tensor'), may hold values from -0.21875 to 0.21875
- text_shrink: bfloat16 [3072, 768], P('tensor'), may hold values from -0.21875 to 0.21875
- visual_prenorm: bfloat16 [768], replicated, may hold values from 0.5 to 1.5
- visual_query: bfloat16 [768, 768], P(None, 'tensor'), may hold values from -0.21875 to 0.21875
- visual_key: bfloat16 [768, 768], P(None, 'tensor'), may hold values from -0.21875 to 0.21875
- visual_value: bfloat16 [768, 768], P(None, 'tensor'), may hold values from -0.21875 to 0.21875
- visual_output: bfloat16 [768, 768], P('tensor'), may hold values from -0.625 to 0.625
- visual_midnorm: bfloat16 [768], replicated, may hold values from 0.5 to 1.5
- visual_expand: bfloat16 [768, 3072], P(None, 'tensor'), may hold values from -0.21875 to 0.21875
- visual_shrink: bfloat16 [3072, 768], P('tensor'), may hold values from -0.21875 to 0.21875
- slopes: float32 [12], P('tensor'), may hold values from 0.5 to 6
- text_cotangent: bfloat16 [16, 512, 768], P('dp', 'tensor'), may hold values from -6 to 6
- visual_cotangent: bfloat16 [16, 512, 768], P('dp', 'tensor'), may hold values from -6 to 6
Outputs:
- text_result: bfloat16 [16, 512, 768], P('dp', 'tensor')
- visual_result: bfloat16 [16, 512, 768], P('dp', 'tensor')
- text_input_grad: bfloat16 [16, 512, 768], P('dp', 'tensor')
- visual_input_grad: bfloat16 [16, 512, 768], P('dp', 'tensor')
- text_prenorm_grad: float32 [768], replicated
- text_query_grad: float32 [768, 768], P(None, 'tensor')
- text_key_grad: float32 [768, 768], P(None, 'tensor')
- text_value_grad: float32 [768, 768], P(None, 'tensor')
- text_output_grad: float32 [768, 768], P('tensor')
- text_midnorm_grad: float32 [768], replicated
- text_expand_grad: float32 [768, 3072], P(None, 'tensor')
- text_shrink_grad: float32 [3072, 768], P('tensor')
- visual_prenorm_grad: float32 [768], replicated
- visual_query_grad: float32 [768, 768], P(None, 'tensor')
- visual_key_grad: float32 [768, 768], P(None, 'tensor')
- visual_value_grad: float32 [768, 768], P(None, 'tensor')
- visual_output_grad: float32 [768, 768], P('tensor')
- visual_midnorm_grad: float32 [768], replicated
- visual_expand_grad: float32 [768, 3072], P(None, 'tensor')
- visual_shrink_grad: float32 [3072, 768], P('tensor')
- slopes_grad: float32 [12], P('tensor')
Inputs may be any that keep to these rules, and one draw needn't show every extreme that they name: `text_count`: each aligned group of 2 pages holds one page with more than 384 text tokens, and one page of all holds exactly 512.
All inputs are finite; a program needn't handle non-finite values.
Results may differ from a plain program's by a relative error of at most 0.023.
Values may be sent and summed in bfloat16 or wider, within the bound.
No kernel may reach another device: no remote copies, remote signals or barrier semaphores. Data moves between devices by JAX's collectives and lax.ppermute only.
A program may use at most 128 MiB of HBM per device.

v0:
```python
import jax
import jax.numpy as jnp
from jax import lax
from jax.sharding import PartitionSpec as P

HEAD_DIM = 64
GRID_W = 32
NBIN = 1000


EPSILON = 1e-05
CONTRACT_ROWS = (((0,), (0,)), ((), ()))
CONTRACT_COLS = (((1,), (1,)), ((), ()))


def layer_norm(values, gain_vector):
    center = values - jnp.mean(values, axis=-1, keepdims=True)
    spread = jnp.mean(center * center, axis=-1, keepdims=True)
    return center * lax.rsqrt(spread + EPSILON) * gain_vector


def gelu_tanh(values):
    return (
        0.5
        * values
        * (1.0 + jnp.tanh(0.7978845608028654 * (values + 0.044715 * values * values * values)))
    )


def pair_distance(coord_x, coord_y):
    delta_x = coord_x[..., :, None] - coord_x[..., None, :]
    delta_y = coord_y[..., :, None] - coord_y[..., None, :]
    return jnp.sqrt(delta_x * delta_x + delta_y * delta_y)


def grid_distance(token_count):
    places = jnp.arange(token_count, dtype=jnp.int32)
    coord_x = ((places % GRID_W).astype(jnp.float32) + 0.5) / GRID_W
    coord_y = ((places // GRID_W).astype(jnp.float32) + 0.5) / (token_count // GRID_W)
    return pair_distance(coord_x, coord_y)


def flatten(blocked):
    return blocked.reshape(-1, blocked.shape[-1])


def score_block(queries, keys_all, distance, key_valid, slopes):
    scores = jnp.einsum("pqhd,pkhd->phqk", queries, keys_all, preferred_element_type=jnp.float32)
    scores = scores * HEAD_DIM ** (-0.5) - slopes[None, :, None, None] * distance[:, None]
    return jnp.where(key_valid[:, None, None, :], scores, -1e30)


def attention_ahead(first_full, weights, distance, key_valid, slopes):
    page_total, token_total, model_width = first_full.shape
    flat_first = flatten(first_full)
    heads_local = weights[1].shape[1] // HEAD_DIM

    def project(matrix):
        product = jnp.dot(flat_first, matrix, preferred_element_type=jnp.float32)
        return product.astype(jnp.bfloat16).reshape(page_total, token_total, heads_local, HEAD_DIM)

    queries = project(weights[1])
    keys_all = project(weights[2])
    values_all = project(weights[3])
    scores = score_block(queries, keys_all, distance, key_valid, slopes)
    highest = jnp.max(scores, axis=-1, keepdims=True)
    exponent = jnp.exp(scores - highest)
    totals = jnp.sum(exponent, axis=-1, keepdims=True)
    soft_weights = (exponent / totals).astype(jnp.bfloat16)
    attended = jnp.einsum(
        "phqk,pkhd->pqhd", soft_weights, values_all, preferred_element_type=jnp.float32
    )
    attended = attended.astype(jnp.bfloat16).reshape(
        page_total * token_total, heads_local * HEAD_DIM
    )
    branch_part = jnp.dot(attended, weights[4], preferred_element_type=jnp.float32).reshape(
        page_total, token_total, model_width
    )
    return (queries, keys_all, values_all, attended, highest + jnp.log(totals), branch_part)


def hidden_ahead(second_full, weights):
    hidden = jnp.dot(flatten(second_full), weights[6], preferred_element_type=jnp.float32)
    active = gelu_tanh(hidden).astype(jnp.bfloat16)
    partial_sum = jnp.dot(active, weights[7], preferred_element_type=jnp.float32).reshape(
        second_full.shape
    )
    return (hidden, active, partial_sum)


def hidden_behind(cotangent_full, second_full, hidden, active, weights):
    flat_cotangent = flatten(cotangent_full)
    shrink_grad = lax.dot_general(
        active, flat_cotangent, CONTRACT_ROWS, preferred_element_type=jnp.float32
    )
    active_grad = lax.dot_general(
        flat_cotangent, weights[7], CONTRACT_COLS, preferred_element_type=jnp.float32
    )
    unused, gelu_back = jax.vjp(gelu_tanh, hidden)
    hidden_grad = gelu_back(active_grad)[0].astype(jnp.bfloat16)
    expand_grad = lax.dot_general(
        flatten(second_full), hidden_grad, CONTRACT_ROWS, preferred_element_type=jnp.float32
    )
    second_part = lax.dot_general(
        hidden_grad, weights[6], CONTRACT_COLS, preferred_element_type=jnp.float32
    )
    return (expand_grad, shrink_grad, second_part.reshape(second_full.shape))


def attention_behind(branch_full, first_full, saved_items, weights, distance, key_valid, slopes):
    queries, keys_all, values_all, attended, log_total, unused = saved_items
    page_total, token_total, model_width = first_full.shape
    flat_first = flatten(first_full)
    flat_branch = flatten(branch_full)
    output_grad = lax.dot_general(
        attended, flat_branch, CONTRACT_ROWS, preferred_element_type=jnp.float32
    )
    attended_grad = lax.dot_general(
        flat_branch, weights[4], CONTRACT_COLS, preferred_element_type=jnp.float32
    )
    attended_grad = attended_grad.astype(jnp.bfloat16).reshape(queries.shape)
    scores = score_block(queries, keys_all, distance, key_valid, slopes)
    probs_full = jnp.exp(scores - log_total)
    soft_weights = probs_full.astype(jnp.bfloat16)
    values_grad = jnp.einsum(
        "phqk,pqhd->pkhd", soft_weights, attended_grad, preferred_element_type=jnp.float32
    ).astype(jnp.bfloat16)
    probs_grad = jnp.einsum(
        "pqhd,pkhd->phqk", attended_grad, values_all, preferred_element_type=jnp.float32
    )
    scores_grad = probs_full * (
        probs_grad - jnp.sum(probs_full * probs_grad, axis=-1, keepdims=True)
    )
    scores_grad = scores_grad.astype(jnp.bfloat16)
    slopes_grad = -jnp.sum(scores_grad.astype(jnp.float32) * distance[:, None], axis=(0, 2, 3))
    queries_grad = jnp.einsum(
        "phqk,pkhd->pqhd", scores_grad, keys_all, preferred_element_type=jnp.float32
    ) * HEAD_DIM ** (-0.5)
    keys_grad = jnp.einsum(
        "phqk,pqhd->pkhd", scores_grad, queries, preferred_element_type=jnp.float32
    ) * HEAD_DIM ** (-0.5)
    queries_grad = flatten(queries_grad.astype(jnp.bfloat16).reshape(page_total * token_total, -1))
    keys_grad = flatten(keys_grad.astype(jnp.bfloat16).reshape(page_total * token_total, -1))
    values_grad = values_grad.reshape(page_total * token_total, -1)
    query_grad = lax.dot_general(
        flat_first, queries_grad, CONTRACT_ROWS, preferred_element_type=jnp.float32
    )
    key_grad = lax.dot_general(
        flat_first, keys_grad, CONTRACT_ROWS, preferred_element_type=jnp.float32
    )
    value_grad = lax.dot_general(
        flat_first, values_grad, CONTRACT_ROWS, preferred_element_type=jnp.float32
    )
    first_part = lax.dot_general(
        queries_grad, weights[1], CONTRACT_COLS, preferred_element_type=jnp.float32
    )
    first_part = first_part + lax.dot_general(
        keys_grad, weights[2], CONTRACT_COLS, preferred_element_type=jnp.float32
    )
    first_part = first_part + lax.dot_general(
        values_grad, weights[3], CONTRACT_COLS, preferred_element_type=jnp.float32
    )
    return (
        query_grad,
        key_grad,
        value_grad,
        output_grad,
        slopes_grad,
        first_part.reshape(page_total, token_total, model_width),
    )


def shards(
    text_input,
    visual_input,
    text_boxes,
    text_count,
    text_prenorm,
    text_query,
    text_key,
    text_value,
    text_output,
    text_midnorm,
    text_expand,
    text_shrink,
    visual_prenorm,
    visual_query,
    visual_key,
    visual_value,
    visual_output,
    visual_midnorm,
    visual_expand,
    visual_shrink,
    slopes,
    text_cotangent,
    visual_cotangent,
):
    page_total = text_boxes.shape[0]
    text_tokens = text_boxes.shape[2]
    visual_tokens = visual_input.shape[1] * lax.axis_size("tensor")
    text_weights = (
        text_prenorm,
        text_query,
        text_key,
        text_value,
        text_output,
        text_midnorm,
        text_expand,
        text_shrink,
    )
    visual_weights = (
        visual_prenorm,
        visual_query,
        visual_key,
        visual_value,
        visual_output,
        visual_midnorm,
        visual_expand,
        visual_shrink,
    )
    text_distance = pair_distance(
        text_boxes[:, 0].astype(jnp.float32) / NBIN, text_boxes[:, 1].astype(jnp.float32) / NBIN
    )
    text_valid = jnp.arange(text_tokens, dtype=jnp.int32)[None, :] < text_count[:, None]
    visual_distance = grid_distance(visual_tokens)[None]
    visual_valid = jnp.full((page_total, visual_tokens), True)
    text_stream = text_input.astype(jnp.float32)
    visual_stream = visual_input.astype(jnp.float32)
    text_gain_first = text_prenorm.astype(jnp.float32)
    text_gain_second = text_midnorm.astype(jnp.float32)
    visual_gain_first = visual_prenorm.astype(jnp.float32)
    visual_gain_second = visual_midnorm.astype(jnp.float32)
    text_first_local = layer_norm(text_stream, text_gain_first).astype(jnp.bfloat16)
    visual_first_local = layer_norm(visual_stream, visual_gain_first).astype(jnp.bfloat16)
    text_first, visual_first = (
        lax.all_gather(text_first_local, "tensor", axis=1, tiled=True),
        lax.all_gather(visual_first_local, "tensor", axis=1, tiled=True),
    )
    text_saved = attention_ahead(text_first, text_weights, text_distance, text_valid, slopes)
    visual_saved = attention_ahead(
        visual_first, visual_weights, visual_distance, visual_valid, slopes
    )
    text_branch, visual_branch = (
        lax.psum_scatter(text_saved[5], "tensor", scatter_dimension=1, tiled=True),
        lax.psum_scatter(visual_saved[5], "tensor", scatter_dimension=1, tiled=True),
    )
    text_middle = text_stream + text_branch
    visual_middle = visual_stream + visual_branch
    text_second_local = layer_norm(text_middle, text_gain_second).astype(jnp.bfloat16)
    visual_second_local = layer_norm(visual_middle, visual_gain_second).astype(jnp.bfloat16)
    text_second, visual_second = (
        lax.all_gather(text_second_local, "tensor", axis=1, tiled=True),
        lax.all_gather(visual_second_local, "tensor", axis=1, tiled=True),
    )
    text_hidden = hidden_ahead(text_second, text_weights)
    visual_hidden = hidden_ahead(visual_second, visual_weights)
    text_added, visual_added = (
        lax.psum_scatter(
            text_hidden[2].astype(jnp.bfloat16), "tensor", scatter_dimension=1, tiled=True
        ).astype(jnp.float32),
        lax.psum_scatter(
            visual_hidden[2].astype(jnp.bfloat16), "tensor", scatter_dimension=1, tiled=True
        ).astype(jnp.float32),
    )
    text_result = (text_middle + text_added).astype(jnp.bfloat16)
    visual_result = (visual_middle + visual_added).astype(jnp.bfloat16)
    text_cot_full, visual_cot_full = (
        lax.all_gather(text_cotangent, "tensor", axis=1, tiled=True),
        lax.all_gather(visual_cotangent, "tensor", axis=1, tiled=True),
    )
    text_hidden_back = hidden_behind(
        text_cot_full, text_second, text_hidden[0], text_hidden[1], text_weights
    )
    visual_hidden_back = hidden_behind(
        visual_cot_full, visual_second, visual_hidden[0], visual_hidden[1], visual_weights
    )
    text_second_grad, visual_second_grad = (
        lax.psum_scatter(text_hidden_back[2], "tensor", scatter_dimension=1, tiled=True),
        lax.psum_scatter(visual_hidden_back[2], "tensor", scatter_dimension=1, tiled=True),
    )
    text_middle_part, text_midnorm_local = jax.vjp(layer_norm, text_middle, text_gain_second)[1](
        text_second_grad
    )
    visual_middle_part, visual_midnorm_local = jax.vjp(
        layer_norm, visual_middle, visual_gain_second
    )[1](visual_second_grad)
    text_middle_grad = text_cotangent.astype(jnp.float32) + text_middle_part
    visual_middle_grad = visual_cotangent.astype(jnp.float32) + visual_middle_part
    text_branch_full, visual_branch_full = (
        lax.all_gather(text_middle_grad.astype(jnp.bfloat16), "tensor", axis=1, tiled=True),
        lax.all_gather(visual_middle_grad.astype(jnp.bfloat16), "tensor", axis=1, tiled=True),
    )
    text_attn_back = attention_behind(
        text_branch_full, text_first, text_saved, text_weights, text_distance, text_valid, slopes
    )
    visual_attn_back = attention_behind(
        visual_branch_full,
        visual_first,
        visual_saved,
        visual_weights,
        visual_distance,
        visual_valid,
        slopes,
    )
    text_first_grad, visual_first_grad = (
        lax.psum_scatter(
            text_attn_back[5].astype(jnp.bfloat16), "tensor", scatter_dimension=1, tiled=True
        ).astype(jnp.float32),
        lax.psum_scatter(
            visual_attn_back[5].astype(jnp.bfloat16), "tensor", scatter_dimension=1, tiled=True
        ).astype(jnp.float32),
    )
    text_stream_part, text_prenorm_local = jax.vjp(layer_norm, text_stream, text_gain_first)[1](
        text_first_grad
    )
    visual_stream_part, visual_prenorm_local = jax.vjp(
        layer_norm, visual_stream, visual_gain_first
    )[1](visual_first_grad)
    text_input_grad = (text_middle_grad + text_stream_part).astype(jnp.bfloat16)
    visual_input_grad = (visual_middle_grad + visual_stream_part).astype(jnp.bfloat16)
    text_prenorm_grad, text_midnorm_grad, visual_prenorm_grad, visual_midnorm_grad = lax.psum(
        (text_prenorm_local, text_midnorm_local, visual_prenorm_local, visual_midnorm_local),
        ("dp", "tensor"),
    )
    slopes_local = text_attn_back[4] + visual_attn_back[4]
    (
        text_query_grad,
        text_key_grad,
        text_value_grad,
        text_output_grad,
        visual_query_grad,
        visual_key_grad,
        visual_value_grad,
        visual_output_grad,
        slopes_grad,
        text_expand_grad,
        text_shrink_grad,
        visual_expand_grad,
        visual_shrink_grad,
    ) = lax.psum(
        (
            text_attn_back[0],
            text_attn_back[1],
            text_attn_back[2],
            text_attn_back[3],
            visual_attn_back[0],
            visual_attn_back[1],
            visual_attn_back[2],
            visual_attn_back[3],
            slopes_local,
            text_hidden_back[0],
            text_hidden_back[1],
            visual_hidden_back[0],
            visual_hidden_back[1],
        ),
        "dp",
    )
    return (
        text_result,
        visual_result,
        text_input_grad,
        visual_input_grad,
        text_prenorm_grad,
        text_query_grad,
        text_key_grad,
        text_value_grad,
        text_output_grad,
        text_midnorm_grad,
        text_expand_grad,
        text_shrink_grad,
        visual_prenorm_grad,
        visual_query_grad,
        visual_key_grad,
        visual_value_grad,
        visual_output_grad,
        visual_midnorm_grad,
        visual_expand_grad,
        visual_shrink_grad,
        slopes_grad,
    )


def solution(mesh):
    return jax.shard_map(
        shards,
        mesh=mesh,
        in_specs=(
            P("dp", "tensor", None),
            P("dp", "tensor", None),
            P("dp", None, None),
            P("dp"),
            P(),
            P(None, "tensor"),
            P(None, "tensor"),
            P(None, "tensor"),
            P("tensor", None),
            P(),
            P(None, "tensor"),
            P("tensor", None),
            P(),
            P(None, "tensor"),
            P(None, "tensor"),
            P(None, "tensor"),
            P("tensor", None),
            P(),
            P(None, "tensor"),
            P("tensor", None),
            P("tensor"),
            P("dp", "tensor", None),
            P("dp", "tensor", None),
        ),
        out_specs=(
            P("dp", "tensor", None),
            P("dp", "tensor", None),
            P("dp", "tensor", None),
            P("dp", "tensor", None),
            P(),
            P(None, "tensor"),
            P(None, "tensor"),
            P(None, "tensor"),
            P("tensor", None),
            P(),
            P(None, "tensor"),
            P("tensor", None),
            P(),
            P(None, "tensor"),
            P(None, "tensor"),
            P(None, "tensor"),
            P("tensor", None),
            P(),
            P(None, "tensor"),
            P("tensor", None),
            P("tensor"),
        ),
        check_vma=False,
    )
```

profile of v0, /device:TPU:0, one launch (start us, length us, event | category | flops | bytes accessed | tf_op | source)
XLA Modules:
  0.0 959.2 jit_solution(17905774407082041619)
XLA Ops:
  11.6 2.0 fusion.58
  17.9 2.0 fusion.59
  21.5 2.1 broadcast_multiply_fusion
  23.6 12.5 %all-gather.13.cloned.1.call-done = bf16[2,512,768]{2,1,0:T(8,128)(2,1)} async-done(((bf16[2,128,768]{2,1,0:T(8,128)(2,1)}), bf16[2,512,768]{2,1,0:T(8,128)(2,1)}) %all-gather.13.cloned.1.call-update) | async-done | bytes 1572880 | tf_op jit(solution)/shard_map/all_gather | solution.py:237
  36.1 2.2 convolution_convert_fusion.4
  38.6 3.0 convolution_convert_fusion.5
  42.9 2.5 convolution_convert_fusion.6
  46.9 3.1 fusion.114
  54.6 2.3 fusion.88
  57.8 2.2 add_sqrt_fusion
  60.0 2.2 convolution_convert_fusion.7
  62.5 3.0 convolution_convert_fusion.8
  66.9 2.5 convolution_convert_fusion.9
  70.7 3.6 fusion.113
  78.2 2.3 fusion.90
  81.8 16.7 %reduce-scatter.13.cloned.1.call-done = f32[2,128,768]{2,1,0:T(8,128)} async-done(((f32[2,512,768]{2,1,0:T(8,128)}), f32[2,128,768]{2,1,0:T(8,128)}) %reduce-scatter.13.cloned.1.call-update) | async-done | bytes 786448 | tf_op jit(solution)/shard_map/reduce_scatter | solution.py:245
  98.5 40.6 %reduce-scatter.9.cloned.1.call-done = f32[2,128,768]{2,1,0:T(8,128)} async-done(((f32[2,512,768]{2,1,0:T(8,128)}), f32[2,128,768]{2,1,0:T(8,128)}) %reduce-scatter.9.cloned.1.call-update) | async-done | bytes 786448 | tf_op jit(solution)/shard_map/reduce_scatter | solution.py:244
  139.1 2.2 fusion.111
  146.2 13.9 %all-gather.21.cloned.1.call-done = bf16[2,512,768]{2,1,0:T(8,128)(2,1)} async-done(((bf16[2,128,768]{2,1,0:T(8,128)(2,1)}), bf16[2,512,768]{2,1,0:T(8,128)(2,1)}) %all-gather.21.cloned.1.call-update) | async-done | bytes 1572880 | tf_op jit(solution)/shard_map/all_gather | solution.py:269
  160.2 4.9 fusion.119
  165.0 16.8 %all-gather.15.cloned.1.call-done = bf16[2,512,768]{2,1,0:T(8,128)(2,1)} async-done(((bf16[2,128,768]{2,1,0:T(8,128)(2,1)}), bf16[2,512,768]{2,1,0:T(8,128)(2,1)}) %all-gather.15.cloned.1.call-update) | async-done | bytes 1572880 | tf_op jit(solution)/shard_map/all_gather | solution.py:253
  181.9 7.1 fusion.11
  188.9 3.1 fusion.120
  193.3 5.0 convolution_convert_fusion
  198.4 4.7 all-gather.17.cloned.1.call-done
  203.1 4.9 fusion.115
  208.1 16.9 %all-gather.11.cloned.1.call-done = bf16[2,512,768]{2,1,0:T(8,128)(2,1)} async-done(((bf16[2,128,768]{2,1,0:T(8,128)(2,1)}), bf16[2,512,768]{2,1,0:T(8,128)(2,1)}) %all-gather.11.cloned.1.call-update) | async-done | bytes 1572880 | tf_op jit(solution)/shard_map/all_gather | solution.py:252
  225.0 7.1 fusion.7
  232.0 3.1 fusion.116
  235.2 5.9 convolution_convert_fusion.1
  243.8 21.7 %reduce-scatter.21.cloned.1.call-done = f32[2,128,768]{2,1,0:T(8,128)} async-done(((f32[2,512,768]{2,1,0:T(8,128)}), f32[2,128,768]{2,1,0:T(8,128)}) %reduce-scatter.21.cloned.1.call-update) | async-done | bytes 786448 | tf_op jit(solution)/shard_map/reduce_scatter | solution.py:279
  265.5 2.0 multiply_reduce_fusion.4
  267.5 29.3 %reduce-scatter.15.cloned.1.call-done = bf16[2,128,768]{2,1,0:T(8,128)(2,1)} async-done(((bf16[2,512,768]{2,1,0:T(8,128)(2,1)}), bf16[2,128,768]{2,1,0:T(8,128)(2,1)}) %reduce-scatter.15.cloned.1.call-update) | async-done | bytes 393232 | tf_op jit(solution)/shard_map/reduce_scatter | solution.py:261
  296.8 2.3 fusion.109
  300.2 4.9 fusion.124
  305.1 3.3 fusion.107
  308.4 28.9 %reduce-scatter.17.cloned.1.call-done = f32[2,128,768]{2,1,0:T(8,128)} async-done(((f32[2,512,768]{2,1,0:T(8,128)}), f32[2,128,768]{2,1,0:T(8,128)}) %reduce-scatter.17.cloned.1.call-update) | async-done | bytes 786448 | tf_op jit(solution)/shard_map/reduce_scatter | solution.py:278
  337.3 2.0 multiply_reduce_fusion.5
  339.3 29.3 %reduce-scatter.11.cloned.1.call-done = bf16[2,128,768]{2,1,0:T(8,128)(2,1)} async-done(((bf16[2,512,768]{2,1,0:T(8,128)(2,1)}), bf16[2,128,768]{2,1,0:T(8,128)(2,1)}) %reduce-scatter.11.cloned.1.call-update) | async-done | bytes 393232 | tf_op jit(solution)/shard_map/reduce_scatter | solution.py:258
  368.6 2.3 fusion.110
  371.9 18.5 %all-gather.23.cloned.1.call-done = bf16[2,512,768]{2,1,0:T(8,128)(2,1)} async-done(((bf16[2,128,768]{2,1,0:T(8,128)(2,1)}), bf16[2,512,768]{2,1,0:T(8,128)(2,1)}) %all-gather.23.cloned.1.call-update) | async-done | bytes 1572880 | tf_op jit(solution)/shard_map/all_gather | solution.py:291
  390.4 2.1 convolution_convert_fusion.2
  393.5 4.7 multiply_reduce_fusion.2
  398.3 2.8 multiply_reduce_fusion
  401.1 1.8 fusion.36
  405.4 6.7 all-gather.19.cloned.1.call-done
  412.1 2.1 convolution_convert_fusion.3
  419.3 3.9 fusion.43
  423.7 4.7 multiply_reduce_fusion.3
  429.7 2.5 multiply_reduce_fusion.1
  436.2 1.9 add_convert_fusion.1
  438.4 4.9 fusion.126
  443.3 3.3 fusion.108
  457.7 22.0 %psum.135 = f32[3]{0:T(128)} all-reduce(f32[3]{0:T(128)S(1)} %negate_add_fusion), channel_id=1, replica_groups=mesh['dp'=8,'tensor'=4] {'dp'}, use_global_device_ids=true, to_apply=%region_52.53 | all-reduce | flops 3 | bytes 24 | tf_op jit(solution)/shard_map/psum | solution.py:340
  479.7 1.9 fusion.65
  484.3 2.1 fusion.61
  487.6 2.1 fusion.60
  489.7 42.9 %all-reduce = (f32[768]{0:T(1024)}, f32[768]{0:T(1024)}, f32[768]{0:T(1024)}, f32[768]{0:T(1024)}) all-reduce(f32[768]{0:T(1024)} %get-tuple-element.27, f32[768]{0:T(1024)} %get-tuple-element.23, f32[768]{0:T(1024)} %get-tuple-element.25, f32[768]{0:T(1024)} %get-tuple-element.21), channel_id=1, replica_groups=mesh['dp'=8,'tensor'=4] {'dp','tensor'}, use_global_device_ids=true, to_apply=%region_31.32 | all-reduce | flops 3072 | bytes 24576 | tf_op jit(solution)/shard_map/psum | solution.py:321
  534.0 1.8 add_convert_fusion.2
  535.9 2.2 add_convert_fusion.3
  538.1 398.5 %all-reduce.4.cloned.1.call-done = (f32[768,192]{0,1:T(8,128)}, f32[768,192]{0,1:T(8,128)}, f32[768,192]{0,1:T(8,128)}, f32[192,768]{1,0:T(8,128)}, f32[768,768]...) async-done(((f32[768,192]{0,1:T(8,128)}, ...) | async-done | bytes 14155792 | tf_op jit(solution)/shard_map/psum | solution.py:340
  936.5 2.1 copy.182
  938.6 1.9 copy.183
  940.5 1.9 copy.184
  (350 shorter events, 78.3 us)
Async XLA Ops:
  7.2 174.7 %copy-start = (bf16[768,768]{1,0:T(8,128)(2,1)S(1)}, bf16[768,768]{1,0:T(8,128)(2,1)}, u32[]{:S(2)}) copy-start(bf16[768,768]{1,0:T(8,128)(2,1)} %param.41) | copy-start | bytes 3538948
  7.2 14.3 %copy-start.94 = (f32[3]{0:T(128)S(1)}, f32[3]{0:T(128)}, u32[]{:S(2)}) copy-start(f32[3]{0:T(128)} %param.43) | copy-start | bytes 40
  7.2 28.9 %all-gather.13.cloned.1.call-start = ((), (), s32[]{:S(2)}) async-start(), calls=%async_computation.12 | async-start | bytes 1966080 | tf_op jit(solution)/shard_map/all_gather | solution.py:237
  13.6 46.4 %all-gather.9.cloned.1.call-start = ((), (), s32[]{:S(2)}) async-start(), calls=%async_computation.8 | async-start | bytes 1966080 | tf_op jit(solution)/shard_map/all_gather | solution.py:236
  17.9 18.2 %copy-start.62 = (bf16[768,192]{0,1:T(8,128)(2,1)S(1)}, bf16[768,192]{0,1:T(8,128)(2,1)}, u32[]{:S(2)}) copy-start(bf16[768,192]{0,1:T(8,128)(2,1)} %param.37) | copy-start | bytes 884740
  20.0 78.6 %reduce-scatter.13.cloned.1.call-start = ((), (), s32[]{:S(2)}) async-start(), calls=%async_computation.13 | async-start | bytes 3932160 | tf_op jit(solution)/shard_map/reduce_scatter | solution.py:245
  36.1 6.8 copy-start.8
  38.6 11.3 %copy-start.20 = (bf16[2,512,3,64]{1,0,3,2:T(2,128)(2,1)}, bf16[2,512,3,64]{1,0,3,2:T(2,128)(2,1)S(1)}, u32[]{:S(2)}) copy-start(bf16[2,512,3,64]{1,0,3,2:T(2,128)(2,1)S(1)} %reshape.409) | copy-start | bytes 1179652
  42.9 7.0 copy-start.22
  56.9 82.2 %reduce-scatter.9.cloned.1.call-start = ((), (), s32[]{:S(2)}) async-start(), calls=%async_computation.9 | async-start | bytes 3932160 | tf_op jit(solution)/shard_map/reduce_scatter | solution.py:244
  60.0 6.8 copy-start.10
  62.5 11.8 %copy-start.46 = (bf16[2,512,3,64]{1,0,3,2:T(2,128)(2,1)}, bf16[2,512,3,64]{1,0,3,2:T(2,128)(2,1)S(1)}, u32[]{:S(2)}) copy-start(bf16[2,512,3,64]{1,0,3,2:T(2,128)(2,1)S(1)} %reshape.404) | copy-start | bytes 1179652
  66.9 7.5 copy-start.44
  78.2 60.9 %copy-start.4 = (bf16[2,128,768]{2,1,0:T(8,128)(2,1)S(1)}, bf16[2,128,768]{2,1,0:T(8,128)(2,1)}, u32[]{:S(2)}) copy-start(bf16[2,128,768]{2,1,0:T(8,128)(2,1)} %param.24) | copy-start | bytes 1179652
  78.2 60.8 %copy-start.6 = (bf16[2,128,768]{2,1,0:T(8,128)(2,1)S(1)}, bf16[2,128,768]{2,1,0:T(8,128)(2,1)}, u32[]{:S(2)}) copy-start(bf16[2,128,768]{2,1,0:T(8,128)(2,1)} %param.23) | copy-start | bytes 1179652
  80.6 79.6 %all-gather.21.cloned.1.call-start = ((), (), s32[]{:S(2)}) async-start(), calls=%async_computation.20 | async-start | bytes 1966080 | tf_op jit(solution)/shard_map/all_gather | solution.py:269
  81.1 100.7 %all-gather.15.cloned.1.call-start = ((), (), s32[]{:S(2)}) async-start(), calls=%async_computation.14 | async-start | bytes 1966080 | tf_op jit(solution)/shard_map/all_gather | solution.py:253
  142.4 60.7 %all-gather.17.cloned.1.call-start = ((), (), s32[]{:S(2)}) async-start(), calls=%async_computation.16 | async-start | bytes 1966080 | tf_op jit(solution)/shard_map/all_gather | solution.py:268
  143.2 81.8 %all-gather.11.cloned.1.call-start = ((), (), s32[]{:S(2)}) async-start(), calls=%async_computation.10 | async-start | bytes 1966080 | tf_op jit(solution)/shard_map/all_gather | solution.py:252
  145.8 119.7 %reduce-scatter.21.cloned.1.call-start = ((), (), s32[]{:S(2)}) async-start(), calls=%async_computation.21 | async-start | bytes 3932160 | tf_op jit(solution)/shard_map/reduce_scatter | solution.py:279
  192.1 104.7 %reduce-scatter.15.cloned.1.call-start = ((), (), s32[]{:S(2)}) async-start(), calls=%async_computation.15 | async-start | bytes 1966080 | tf_op jit(solution)/shard_map/reduce_scatter | solution.py:261
  198.3 138.9 %reduce-scatter.17.cloned.1.call-start = ((), (), s32[]{:S(2)}) async-start(), calls=%async_computation.17 | async-start | bytes 3932160 | tf_op jit(solution)/shard_map/reduce_scatter | solution.py:278
  203.1 21.8 %copy-start.99 = (bf16[768,768]{1,0:T(8,128)(2,1)S(1)}, bf16[768,768]{1,0:T(8,128)(2,1)}, u32[]{:S(2)}) copy-start(bf16[768,768]{1,0:T(8,128)(2,1)} %param.33) | copy-start | bytes 3538948
  235.1 133.4 %reduce-scatter.11.cloned.1.call-start = ((), (), s32[]{:S(2)}) async-start(), calls=%async_computation.11 | async-start | bytes 1966080 | tf_op jit(solution)/shard_map/reduce_scatter | solution.py:258
  235.2 6.1 copy-start.41
  241.1 24.4 %copy-start.72 = (f32[768]{0:T(1024)S(1)}, f32[768]{0:T(1024)}, u32[]{:S(2)}) copy-start(f32[768]{0:T(1024)} %convert_element_type.271) | copy-start | bytes 9220
  241.1 149.3 %all-gather.23.cloned.1.call-start = ((), (), s32[]{:S(2)}) async-start(), calls=%async_computation.22 | async-start | bytes 1966080 | tf_op jit(solution)/shard_map/all_gather | solution.py:291
  242.6 56.5 %copy-start.26 = (bf16[2,128,768]{2,1,0:T(8,128)(2,1)S(1)}, bf16[2,128,768]{2,1,0:T(8,128)(2,1)}, u32[]{:S(2)}) copy-start(bf16[2,128,768]{2,1,0:T(8,128)(2,1)} %param.45) | copy-start | bytes 1179652
  243.8 56.3 %copy-start.74 = (f32[2,3,512]{2,1,0:T(4,128)S(1)}, f32[2,3,512]{2,1,0:T(4,128)}, u32[]{:S(2)}) copy-start(f32[2,3,512]{2,1,0:T(4,128)} %copy-done.73) | copy-start | bytes 36868
  243.8 56.3 %copy-start.78 = (f32[2,3,512]{2,1,0:T(4,128)S(1)}, f32[2,3,512]{2,1,0:T(4,128)}, u32[]{:S(2)}) copy-start(f32[2,3,512]{2,1,0:T(4,128)} %copy-done.77) | copy-start | bytes 36868
  299.1 6.0 copy-start.15
  299.1 6.0 copy-start.89
  300.1 112.0 %all-gather.19.cloned.1.call-start = ((), (), s32[]{:S(2)}) async-start(), calls=%async_computation.18 | async-start | bytes 1966080 | tf_op jit(solution)/shard_map/all_gather | solution.py:290
  300.2 4.9 copy-start.97
  300.2 4.9 copy-start.101
  308.4 62.5 %copy-start.28 = (bf16[2,128,768]{2,1,0:T(8,128)(2,1)S(1)}, bf16[2,128,768]{2,1,0:T(8,128)(2,1)}, u32[]{:S(2)}) copy-start(bf16[2,128,768]{2,1,0:T(8,128)(2,1)} %param.44) | copy-start | bytes 1179652
  308.4 82.1 %copy-start.58 = (bf16[192,768]{1,0:T(8,128)(2,1)S(1)}, bf16[192,768]{1,0:T(8,128)(2,1)}, u32[]{:S(2)}) copy-start(bf16[192,768]{1,0:T(8,128)(2,1)} %param.39) | copy-start | bytes 884740
  370.9 21.6 %copy-start.17 = (f32[2,128,768]{2,1,0:T(8,128)}, f32[2,128,768]{2,1,0:T(8,128)S(1)}, u32[]{:S(2)}) copy-start(f32[2,128,768]{2,1,0:T(8,128)S(1)} %get-tuple-element.52) | copy-start | bytes 2359300
  370.9 19.6 %copy-start.90 = (f32[2,128]{1,0:T(2,128)}, f32[2,128]{1,0:T(2,128)S(1)}, u32[]{:S(2)}) copy-start(f32[2,128]{1,0:T(2,128)S(1)} %negate_multiply_fusion.3) | copy-start | bytes 3076
  371.9 107.8 %reduce-scatter.23.cloned.1.call-start = ((), (), s32[]{:S(2)}) async-start(), calls=%async_computation.23 | async-start | bytes 1966080 | tf_op jit(solution)/shard_map/reduce_scatter | solution.py:309
  392.5 5.7 slice-start
  404.3 7.8 copy-start.60
  405.4 9.5 copy-start.49
  405.4 10.0 %copy-start.48 = (bf16[2,512,3,64]{1,3,2,0:T(8,128)(2,1)S(1)}, bf16[2,512,3,64]{1,3,2,0:T(8,128)(2,1)}, u32[]{:S(2)}) copy-start(bf16[2,512,3,64]{1,3,2,0:T(8,128)(2,1)} %fusion.36) | copy-start | bytes 1179652
  419.0 62.6 %reduce-scatter.19.cloned.1.call-start = ((), (), s32[]{:S(2)}) async-start(), calls=%async_computation.19 | async-start | bytes 1966080 | tf_op jit(solution)/shard_map/reduce_scatter | solution.py:306
  423.6 4.8 slice-start.2
  423.7 5.4 slice-start.3
  423.7 6.0 copy-start.14
  438.0 498.5 %all-reduce.4.cloned.1.call-start = ((), (), s32[]{:S(2)}) async-start(), calls=%async_computation.24 | async-start | bytes 28311552 | tf_op jit(solution)/shard_map/psum | solution.py:340
  438.4 4.9 copy-start.96
  438.4 4.9 copy-start.100
  457.0 22.7 %copy-start.5 = (bf16[2,128,768]{2,1,0:T(8,128)(2,1)S(1)}, bf16[2,128,768]{2,1,0:T(8,128)(2,1)}, u32[]{:S(2)}) copy-start(bf16[2,128,768]{2,1,0:T(8,128)(2,1)} %param.24) | copy-start | bytes 1179652
  457.0 22.7 %copy-start.68 = (f32[768]{0:T(1024)S(1)}, f32[768]{0:T(1024)}, u32[]{:S(2)}) copy-start(f32[768]{0:T(1024)} %copy-done.67) | copy-start | bytes 9220
  457.0 22.7 %copy-start.80 = (f32[2,128]{1,0:T(2,128)S(1)}, f32[2,128]{1,0:T(2,128)}, u32[]{:S(2)}) copy-start(f32[2,128]{1,0:T(2,128)} %copy-done.79) | copy-start | bytes 3076
  457.0 24.6 %copy-start.7 = (bf16[2,128,768]{2,1,0:T(8,128)(2,1)S(1)}, bf16[2,128,768]{2,1,0:T(8,128)(2,1)}, u32[]{:S(2)}) copy-start(bf16[2,128,768]{2,1,0:T(8,128)(2,1)} %param.23) | copy-start | bytes 1179652
  457.1 24.6 %copy-start.70 = (f32[768]{0:T(1024)S(1)}, f32[768]{0:T(1024)}, u32[]{:S(2)}) copy-start(f32[768]{0:T(1024)} %copy-done.69) | copy-start | bytes 9220
  457.1 24.6 %copy-start.82 = (f32[2,128]{1,0:T(2,128)S(1)}, f32[2,128]{1,0:T(2,128)}, u32[]{:S(2)}) copy-start(f32[2,128]{1,0:T(2,128)} %copy-done.81) | copy-start | bytes 3076
  457.1 76.9 %copy-start.16 = (f32[2,128,768]{2,1,0:T(8,128)S(1)}, f32[2,128,768]{2,1,0:T(8,128)}, u32[]{:S(2)}) copy-start(f32[2,128,768]{2,1,0:T(8,128)} %copy-done.15) | copy-start | bytes 2359300
  457.1 76.9 %copy-start.27 = (bf16[2,128,768]{2,1,0:T(8,128)(2,1)S(1)}, bf16[2,128,768]{2,1,0:T(8,128)(2,1)}, u32[]{:S(2)}) copy-start(bf16[2,128,768]{2,1,0:T(8,128)(2,1)} %param.45) | copy-start | bytes 1179652
  457.1 78.8 %copy-start.18 = (f32[2,128,768]{2,1,0:T(8,128)S(1)}, f32[2,128,768]{2,1,0:T(8,128)}, u32[]{:S(2)}) copy-start(f32[2,128,768]{2,1,0:T(8,128)} %copy-done.17) | copy-start | bytes 2359300
  479.7 54.3 %copy-start.24 = (bf16[2,128,768]{2,1,0:T(8,128)(2,1)S(1)}, bf16[2,128,768]{2,1,0:T(8,128)(2,1)}, u32[]{:S(2)}) copy-start(bf16[2,128,768]{2,1,0:T(8,128)(2,1)} %reduce-scatter.23.cloned.1.call-done) | copy-start | bytes 1179652
  481.7 54.2 %copy-start.25 = (bf16[2,128,768]{2,1,0:T(8,128)(2,1)S(1)}, bf16[2,128,768]{2,1,0:T(8,128)(2,1)}, u32[]{:S(2)}) copy-start(bf16[2,128,768]{2,1,0:T(8,128)(2,1)} %reduce-scatter.19.cloned.1.call-done) | copy-start | bytes 1179652
  936.5 5.9 copy-start.54
  936.5 6.7 copy-start.32
  (61 other events, 137.1 us)
Sparse Core Ops, SparseCore 0:
  13.7 22.3 all-gather.12
  38.3 19.7 all-gather.8
  60.5 37.9 reduce-scatter.12
  101.1 37.9 reduce-scatter.8
  140.5 19.6 all-gather.20
  162.2 19.6 all-gather.14
  183.4 19.6 all-gather.16
  205.3 19.6 all-gather.10
  227.5 37.9 reduce-scatter.20
  268.6 28.1 reduce-scatter.14
  299.3 37.9 reduce-scatter.16
  340.4 28.1 reduce-scatter.10
  370.7 19.6 all-gather.22
  392.4 19.6 all-gather.18
  419.1 28.1 reduce-scatter.22
  449.9 28.1 reduce-scatter.18
  486.1 450.4 all-reduce.3
where the time goes:
time: 966 us; the launch traced here: 959 us
  waiting for transfers between devices  656 us (68%)
  matrix products  126 us (13%)
  blocking collectives  65 us (7%)
  other arithmetic  54 us (6%)
  local copies, waits for them, and re-layouts  40.1 us (4%)
  between operations  15.6 us (2%)
    psum x1, waiting for transfers between devices, shards(): lax.psum((text_attn_back[0], text_attn_back[1], text_attn_back[2], text_a...  398 us
    psum x1, blocking collectives, shards(): lax.psum((text_prenorm_local, text_midnorm_local, visual_prenorm_local, v...  42.9 us
    reduce_scatter x1, waiting for transfers between devices, shards(): lax.psum_scatter(text_saved[5], 'tensor', scatter_dimension=1, tiled=True)  40.6 us
    unnamed x238, local copies, waits for them, and re-layouts  29.6 us
    reduce_scatter x1, waiting for transfers between devices, shards(): lax.psum_scatter(text_hidden[2].astype(jnp.bfloat16), 'tensor', scatter_d...  29.3 us
    reduce_scatter x1, waiting for transfers between devices, shards(): lax.psum_scatter(visual_hidden[2].astype(jnp.bfloat16), 'tensor', scatter...  29.3 us
    reduce_scatter x1, waiting for transfers between devices, shards(): lax.psum_scatter(text_hidden_back[2], 'tensor', scatter_dimension=1, tile...  28.9 us
    psum x1, blocking collectives, shards(): lax.psum((text_attn_back[0], text_attn_back[1], text_attn_back[2], text_a...  22 us
  transfers between devices with their start and end apart: 17, of which 14 were waited for; matrix products, arithmetic and copies ran while one was open for 19% of the time, Pallas kernels for 0%

commit v1 on v0

v1 whole, which is shorter than its diff:
```python
import jax
import jax.numpy as jnp
from jax import lax
from jax.sharding import PartitionSpec as P

HEAD_DIM = 64
GRID_W = 32
NBIN = 1000
EPSILON = 1e-05
AXES = ("dp", "tensor")
ROWS = (((0,), (0,)), ((), ()))
COLS = (((1,), (1,)), ((), ()))
F32 = jnp.float32
BF16 = jnp.bfloat16


def layer_norm(values, gain):
    center = values - jnp.mean(values, axis=-1, keepdims=True)
    spread = jnp.mean(center * center, axis=-1, keepdims=True)
    return center * lax.rsqrt(spread + EPSILON) * gain


def gelu_tanh(values):
    return (
        0.5
        * values
        * (1.0 + jnp.tanh(0.7978845608028654 * (values + 0.044715 * values * values * values)))
    )


def matmul(a, b, dims=None):
    if dims is None:
        return jnp.dot(a, b, preferred_element_type=F32)
    return lax.dot_general(a, b, dims, preferred_element_type=F32)


class Links:
    def __init__(self, pairs):
        self.pairs = pairs
        self.high = pairs // 2
        self.ring_size = 4

    def table(self, move):
        out = []
        for dp in range(self.pairs):
            for tensor in range(4):
                hi, lo, x, c = move(dp // 2, dp % 2, tensor // 2, tensor % 2)
                out.append((dp * 4 + tensor, (hi * 2 + lo) * 4 + x * 2 + c))
        return out

    def send(self, value, move):
        return lax.ppermute(value, AXES, self.table(move))

    def core(self, value):
        return self.send(value, lambda hi, lo, x, c: (hi, lo, x, 1 - c))

    def across(self, value):
        return self.send(value, lambda hi, lo, x, c: (hi, lo, 1 - x, c))

    def stream(self, value):
        return self.send(value, lambda hi, lo, x, c: (hi, 1 - lo, x, c))

    def level(self, value, bit):
        return self.send(value, lambda hi, lo, x, c: (hi ^ bit, lo, x, c))

    def ring(self, value):
        n = self.ring_size
        return self.send(
            value, lambda hi, lo, x, c: (hi // n * n + (hi % n + 1) % n, lo, x, c)
        )

    def out_to_page(self, value, k):
        return self.send(value, lambda hi, lo, x, c: (hi, c ^ (k & 1), x ^ (k >> 1), lo))

    def back_to_rows(self, value, k):
        return self.send(value, lambda hi, lo, x, c: (hi, c, x ^ (k >> 1), lo ^ (k & 1)))


def add_low(a, b):
    return (a.astype(F32) + b.astype(F32)).astype(BF16)


def pick(flag, one, other):
    return jnp.where(flag, one, other)


def shards(
    text_input,
    visual_input,
    text_boxes,
    text_count,
    text_prenorm,
    text_query,
    text_key,
    text_value,
    text_output,
    text_midnorm,
    text_expand,
    text_shrink,
    visual_prenorm,
    visual_query,
    visual_key,
    visual_value,
    visual_output,
    visual_midnorm,
    visual_expand,
    visual_shrink,
    slopes,
    text_cotangent,
    visual_cotangent,
):
    dp_index = lax.axis_index("dp")
    tensor_index = lax.axis_index("tensor")
    hi, lo = dp_index // 2, dp_index % 2
    x, c = tensor_index // 2, tensor_index % 2
    links = Links(lax.axis_size("dp"))
    block = text_input.shape[1]
    tokens = text_boxes.shape[2]
    width = text_input.shape[2]
    heads_slot = slopes.shape[0]
    is_text = lo == 0
    place = 2 * x + lo

    def to_page(text_rows, visual_rows):
        both = jnp.stack([text_rows, visual_rows])
        parts = []
        for k in range(4):
            part = lax.dynamic_slice(
                both, (c ^ (k & 1), x ^ (k >> 1), 0, 0), (1, 1, block, width)
            ).reshape(block, width)
            parts.append(links.out_to_page(part, k))
        return jnp.concatenate(parts, axis=0)

    def to_rows(page):
        parts = [
            links.back_to_rows(page[k * block : (k + 1) * block], k) for k in range(4)
        ]
        even = [pick(c == 0, parts[2 * k2], parts[2 * k2 + 1]) for k2 in range(2)]
        odd = [pick(c == 0, parts[2 * k2 + 1], parts[2 * k2]) for k2 in range(2)]
        text = jnp.stack([pick(x == 0, even[0], even[1]), pick(x == 0, even[1], even[0])])
        visual = jnp.stack([pick(x == 0, odd[0], odd[1]), pick(x == 0, odd[1], odd[0])])
        return text, visual

    source = to_page(text_input, visual_input)
    info = jnp.concatenate(
        [
            lax.dynamic_slice(text_boxes, (x, 0, 0), (1, 2, tokens)).reshape(2, tokens),
            jnp.full((1, tokens), lax.dynamic_slice(text_count, (x,), (1,))[0], jnp.int32),
        ]
    )
    info = pick(c == lo, info, links.stream(info))
    count = pick(is_text, info[2, 0], tokens)
    order = jnp.arange(tokens, dtype=jnp.int32)
    absolute = (place ^ (order // block)) * block + order % block
    boxes = info[:2].reshape(2, 4, block)
    boxes = pick(place // 2 == 1, boxes[:, jnp.array([2, 3, 0, 1])], boxes)
    boxes = pick(place % 2 == 1, boxes[:, jnp.array([1, 0, 3, 2])], boxes)
    boxes = boxes.reshape(2, tokens).astype(F32) / NBIN
    coord_x = pick(is_text, boxes[0], ((absolute % GRID_W).astype(F32) + 0.5) / GRID_W)
    coord_y = pick(
        is_text, boxes[1], ((absolute // GRID_W).astype(F32) + 0.5) / (tokens // GRID_W)
    )
    delta_x = coord_x[:, None] - coord_x[None, :]
    delta_y = coord_y[:, None] - coord_y[None, :]
    distance = jnp.sqrt(delta_x * delta_x + delta_y * delta_y)
    valid = absolute < count

    half = hi % 2

    def slots(shard):
        rows = shard.shape[0] // 2
        mine = lax.dynamic_slice(shard, (half * rows, 0), (rows, shard.shape[1]))
        first = links.across(mine)
        second = links.level(first, 1)
        other = pick(
            half == 0,
            jnp.concatenate([first, second]),
            jnp.concatenate([second, first]),
        )
        return [shard, links.core(shard), other, links.core(other)]

    qkv_weights = slots(
        pick(
            is_text,
            jnp.concatenate([text_query, text_key, text_value], axis=1),
            jnp.concatenate([visual_query, visual_key, visual_value], axis=1),
        )
    )
    slopes_other = links.across(slopes)
    slope_slots = [slopes, links.core(slopes), slopes_other, links.core(slopes_other)]
    cotangent = to_page(text_cotangent, visual_cotangent)
    output_weights = slots(pick(is_text, text_output, visual_output))
    expand_weights = slots(pick(is_text, text_expand, visual_expand))
    shrink_weights = slots(pick(is_text, text_shrink, visual_shrink))
    gain_first = pick(is_text, text_prenorm, visual_prenorm).astype(F32)
    gain_second = pick(is_text, text_midnorm, visual_midnorm).astype(F32)

    def split(packed):
        parts = jnp.split(packed, 3, axis=1)
        return [part.reshape(tokens, heads_slot, HEAD_DIM) for part in parts]

    def scores_of(queries, keys_all, slope):
        scores = jnp.einsum("qhd,khd->hqk", queries, keys_all, preferred_element_type=F32)
        scores = scores * HEAD_DIM ** (-0.5) - slope[:, None, None] * distance[None]
        return jnp.where(valid[None, None, :], scores, -1e30)

    stream = source.astype(F32)
    first_normed = layer_norm(stream, gain_first).astype(BF16)
    heads = []
    attended = []
    branch = None
    for j in range(4):
        packed = matmul(first_normed, qkv_weights[j]).astype(BF16)
        queries, keys_all, values_all = split(packed)
        scores = scores_of(queries, keys_all, slope_slots[j])
        highest = jnp.max(scores, axis=-1, keepdims=True)
        exponent = jnp.exp(scores - highest)
        totals = jnp.sum(exponent, axis=-1, keepdims=True)
        soft_weights = (exponent / totals).astype(BF16)
        mixed = jnp.einsum("hqk,khd->qhd", soft_weights, values_all, preferred_element_type=F32)
        mixed = mixed.astype(BF16).reshape(tokens, -1)
        heads.append((queries, keys_all, values_all, highest + jnp.log(totals)))
        attended.append(mixed)
        part = matmul(mixed, output_weights[j])
        branch = part if branch is None else branch + part
    middle = stream + branch
    second_normed = layer_norm(middle, gain_second).astype(BF16)
    hidden = [matmul(second_normed, expand_weights[j]) for j in range(4)]
    active = [gelu_tanh(h).astype(BF16) for h in hidden]

    def reduced(parts):
        own = add_low(parts[0], links.core(parts[1]))
        far = add_low(parts[2], links.core(parts[3]))
        own = add_low(own, links.across(far))
        n = links.ring_size
        place_ring = hi % n
        rows = own.shape[0] // n

        def piece(index):
            return lax.dynamic_slice(own, (index % n * rows, 0), (rows, own.shape[1]))

        moving = piece(place_ring + n - 1)
        for k in range(n - 1):
            moving = add_low(links.ring(moving), piece(place_ring + n - 2 - k + n))
        groups = links.high // n
        if groups > 1:
            group_table = [
                [(g * n + r) * 2 + l for g in range(groups)] for r in range(n) for l in range(2)
            ]
            moving = lax.psum(moving, "dp", axis_index_groups=group_table)
        chunks = [moving]
        for k in range(n - 1):
            chunks.append(links.ring(chunks[-1]))
        theirs = [links.stream(chunk) for chunk in chunks]

        def laid(flag):
            cycle = [pick(flag, a, b) for a, b in zip(chunks, theirs, strict=True)][::-1]
            both = jnp.concatenate(cycle + cycle)
            start = (n - 1 - place_ring) * rows
            return lax.dynamic_slice(both, (start, 0), own.shape).astype(F32)

        return laid(is_text), laid(jnp.logical_not(is_text))

    shrink_grads = reduced([matmul(a, cotangent, ROWS).astype(BF16) for a in active])
    added = None
    hidden_grad = []
    second_grad = None
    for j in range(4):
        part = matmul(active[j], shrink_weights[j])
        added = part if added is None else added + part
        active_grad = matmul(cotangent, shrink_weights[j], COLS)
        back = jax.vjp(gelu_tanh, hidden[j])[1](active_grad)[0].astype(BF16)
        hidden_grad.append(back)
        part = matmul(back, expand_weights[j], COLS)
        second_grad = part if second_grad is None else second_grad + part
    result = (middle + added).astype(BF16)
    text_result, visual_result = to_rows(result)
    expand_grads = reduced([matmul(second_normed, h, ROWS).astype(BF16) for h in hidden_grad])
    middle_part, midnorm_grad = jax.vjp(layer_norm, middle, gain_second)[1](second_grad)
    middle_grad = cotangent.astype(F32) + middle_part
    branch_grad = middle_grad.astype(BF16)

    output_grads = reduced([matmul(a, branch_grad, ROWS).astype(BF16) for a in attended])
    qkv_grads = []
    slope_grads = []
    first_grad = None
    for j in range(4):
        queries, keys_all, values_all, log_total = heads[j]
        attended_grad = matmul(branch_grad, output_weights[j], COLS).astype(BF16)
        attended_grad = attended_grad.reshape(tokens, heads_slot, HEAD_DIM)
        probs = jnp.exp(scores_of(queries, keys_all, slope_slots[j]) - log_total)
        values_grad = jnp.einsum(
            "hqk,qhd->khd", probs.astype(BF16), attended_grad, preferred_element_type=F32
        )
        probs_grad = jnp.einsum(
            "qhd,khd->hqk", attended_grad, values_all, preferred_element_type=F32
        )
        scores_grad = probs * (probs_grad - jnp.sum(probs * probs_grad, axis=-1, keepdims=True))
        scores_grad = scores_grad.astype(BF16)
        slope_grads.append(-jnp.sum(scores_grad.astype(F32) * distance[None], axis=(1, 2)))
        queries_grad = jnp.einsum(
            "hqk,khd->qhd", scores_grad, keys_all, preferred_element_type=F32
        ) * HEAD_DIM ** (-0.5)
        keys_grad = jnp.einsum(
            "hqk,qhd->khd", scores_grad, queries, preferred_element_type=F32
        ) * HEAD_DIM ** (-0.5)
        packed = jnp.concatenate(
            [g.astype(BF16).reshape(tokens, -1) for g in (queries_grad, keys_grad, values_grad)],
            axis=1,
        )
        qkv_grads.append(matmul(first_normed, packed, ROWS).astype(BF16))
        part = matmul(packed, qkv_weights[j], COLS)
        first_grad = part if first_grad is None else first_grad + part
    qkv_text, qkv_visual = reduced(qkv_grads)
    stream_part, prenorm_grad = jax.vjp(layer_norm, stream, gain_first)[1](first_grad)
    text_input_grad, visual_input_grad = to_rows((middle_grad + stream_part).astype(BF16))

    slope_rel = jnp.stack(slope_grads)
    slope_rel = pick(c == 0, slope_rel, slope_rel[jnp.array([1, 0, 3, 2])])
    slope_abs = pick(x == 0, slope_rel, slope_rel[jnp.array([2, 3, 0, 1])]).reshape(-1)
    slope_row = jnp.zeros((width,), F32).at[: slope_abs.shape[0]].set(slope_abs)
    small = jnp.stack([prenorm_grad, midnorm_grad, slope_row])
    small = small + links.core(small)
    small = small + links.across(small)
    bit = 1
    while bit < links.high:
        small = small + links.level(small, bit)
        bit *= 2
    small_other = links.stream(small)
    text_small = pick(is_text, small, small_other)
    visual_small = pick(is_text, small_other, small)
    slope_sum = lax.dynamic_slice(
        (text_small + visual_small)[2], (tensor_index * heads_slot,), (heads_slot,)
    )
    text_qkv = jnp.split(qkv_text, 3, axis=1)
    visual_qkv = jnp.split(qkv_visual, 3, axis=1)
    return (
        text_result,
        visual_result,
        text_input_grad,
        visual_input_grad,
        text_small[0],
        *text_qkv,
        output_grads[0],
        text_small[1],
        expand_grads[0],
        shrink_grads[0],
        visual_small[0],
        *visual_qkv,
        output_grads[1],
        visual_small[1],
        expand_grads[1],
        shrink_grads[1],
        slope_sum,
    )


def solution(mesh):
    rows = P("dp", "tensor", None)
    split_out = P(None, "tensor")
    split_in = P("tensor", None)
    weights = (P(), split_out, split_out, split_out, split_in, P(), split_out, split_in)
    return jax.shard_map(
        shards,
        mesh=mesh,
        in_specs=(
            rows,
            rows,
            P("dp", None, None),
            P("dp"),
            *weights,
            *weights,
            P("tensor"),
            rows,
            rows,
        ),
        out_specs=(rows, rows, rows, rows, *weights, *weights, P("tensor")),
        check_vma=False,
    )
```

time: 966 us -> 517 us (0.54)
  waiting for transfers between devices: 656 us -> 261 us
  starting transfers between devices: 1.95 us -> 72.9 us
  blocking collectives: 65 us -> 0 us
  matrix products: 126 us -> 89.9 us
  local copies, waits for them, and re-layouts: 40.1 us -> 26.7 us
  between operations: 15.6 us -> 4.2 us
    psum x1 -> x0, waiting for transfers between devices: 398 us -> none  [shards(): lax.psum((text_attn_back[0], text_attn_back[1], text_attn_back[2], text_a...]
    ppermute x0 -> x93, waiting for transfers between devices: none -> 261 us  [send(): return lax.ppermute(value, AXES, self.table(move))]
    reduce_scatter x8 -> x0, waiting for transfers between devices: 166 us -> none  [the longest x1 40.6 us: shards(): lax.psum_scatter(text_saved[5], 'tensor', scatter_dimension=1, tiled=True)]
    all_gather x8 -> x0, waiting for transfers between devices: 90.1 us -> none  [the longest x1 18.5 us: shards(): lax.all_gather(visual_middle_grad.astype(jnp.bfloat16), 'tensor', axis=1,...]
    ppermute x0 -> x93, starting transfers between devices: none -> 72.9 us  [send(): return lax.ppermute(value, AXES, self.table(move))]
    psum x2 -> x0, blocking collectives: 65 us -> none  [the longest x1 42.9 us: shards(): lax.psum((text_prenorm_local, text_midnorm_local, visual_prenorm_local, v...]
    dot_general x48 -> x72, matrix products: 126 us -> 89.9 us  [the longest x32 39.2 us: matmul(): return lax.dot_general(a, b, dims, preferred_element_type=F32)]
    unnamed x238 -> x243, local copies, waits for them, and re-layouts: 29.6 us -> 10.4 us
  transfers between devices with their start and end apart: 17 -> 93, of which waited for: 14 -> 45; matrix products, arithmetic and copies ran while one was open for 19% -> 20% of each run, Pallas kernels for 0% -> 0%
where the time goes in v1:
time: 517 us; the launch traced here: 512 us
  waiting for transfers between devices  261 us (50%)
  matrix products  89.9 us (17%)
  starting transfers between devices  72.9 us (14%)
  other arithmetic  57.8 us (11%)
  local copies, waits for them, and re-layouts  26.7 us (5%)
    ppermute x93, waiting for transfers between devices, send(): return lax.ppermute(value, AXES, self.table(move))  261 us
    ppermute x93, starting transfers between devices, send(): return lax.ppermute(value, AXES, self.table(move))  72.9 us
    dot_general x32, matrix products, matmul(): return lax.dot_general(a, b, dims, preferred_element_type=F32)  39.2 us
    dot_general x16, matrix products, matmul(): return jnp.dot(a, b, preferred_element_type=F32)  18.3 us
    unnamed x30, other arithmetic  15.8 us
    unnamed x243, local copies, waits for them, and re-layouts  10.4 us
  transfers between devices with their start and end apart: 93, of which 45 were waited for; matrix products, arithmetic and copies ran while one was open for 20% of the time, Pallas kernels for 0%

profile of v1, /device:TPU:0, one launch (start us, length us, event | category | flops | bytes accessed | tf_op | source)
XLA Modules:
  0.0 512.5 jit_solution(16636699475968808872)
XLA Ops:
  2.9 3.0 collective-permute-start.4
  40.5 4.1 collective-permute-done.8
  46.3 26.7 %collective-permute-done.30 = bf16[128,768]{1,0:T(8,128)(2,1)S(1)} collective-permute-done((bf16[128,768]{1,0:T(8,128)(2,1)S(1)}, bf16[128,768]{1,0:T(8,128)(2,1)S(1)}, u32[]{:S(2)}, u32[]{:S(2)}) %collective-permute-start.30) | collective-permute-done | bytes 196640 | tf_op jit(solution)/shard_map/ppermute | solution.py:52
  74.6 4.9 collective-permute-done.12
  86.3 11.4 %collective-permute-done.19 = bf16[384,768]{1,0:T(8,128)(2,1)S(1)} collective-permute-done((bf16[384,768]{1,0:T(8,128)(2,1)S(1)}, bf16[384,768]{1,0:T(8,128)(2,1)S(1)}, u32[]{:S(2)}, u32[]{:S(2)}) %collective-permute-start.19) | collective-permute-done | bytes 589856 | tf_op jit(solution)/shard_map/ppermute | solution.py:52
  98.2 11.7 %collective-permute-done.21 = bf16[384,768]{1,0:T(8,128)(2,1)S(1)} collective-permute-done((bf16[384,768]{1,0:T(8,128)(2,1)S(1)}, bf16[384,768]{1,0:T(8,128)(2,1)S(1)}, u32[]{:S(2)}, u32[]{:S(2)}) %collective-permute-start.21) | collective-permute-done | bytes 589856 | tf_op jit(solution)/shard_map/ppermute | solution.py:52
  113.2 2.3 fusion.190
  123.5 2.0 convolution_convert_fusion.1
  125.5 2.0 fusion.210
  127.6 2.0 convolution_convert_fusion.2
  129.6 2.0 convolution_convert_fusion.3
  131.6 2.2 fusion.185
  135.6 3.3 fusion.23
  138.9 2.3 convolution_convert_fusion.6
  142.0 2.1 fusion.214
  144.1 3.5 fusion.186
  150.3 2.0 convolution_convert_fusion
  152.3 3.0 fusion.31
  164.4 2.3 multiply_reduce_fusion.7
  168.6 2.3 multiply_reduce_fusion.6
  172.2 2.4 multiply_reduce_fusion.5
  176.3 2.3 multiply_reduce_fusion.4
  178.6 8.3 %multiply_reduce_fusion.3 = (f32[3]{0:T(128)S(1)}, f32[3]{0:T(128)S(1)}, f32[3]{0:T(128)S(1)}, f32[3]{0:T(128)S(1)}, bf16[3,512,512]{1,2,0:T(8,128)(2,1)}, /*ind...) fusion(f32[512,512]{0,1:T(8,128)S(1)} %add_sqrt_fusion, ...), kind=kLoop, calls=%fused_computation.7 | loop fusion | flops 22020084 | bytes 32555056 | tf_op jit(solution)/shard_map/reduce_sum | solution.py:300
  187.0 2.9 fusion.72
  197.4 2.5 fusion.187
  213.6 3.3 collective-permute-start.36
  220.7 2.2 collective-permute-done.37
  226.7 2.6 collective-permute-start.39
  232.5 2.7 collective-permute-done.40
  242.0 5.1 %collective-permute-done.56 = bf16[192,768]{1,0:T(8,128)(2,1)S(1)} collective-permute-done((bf16[192,768]{1,0:T(8,128)(2,1)S(1)}, bf16[192,768]{1,0:T(8,128)(2,1)S(1)}, u32[]{:S(2)}, u32[]{:S(2)}) %collective-permute-start.56) | collective-permute-done | bytes 294944 | tf_op jit(solution)/shard_map/ppermute | solution.py:52
  248.2 3.5 collective-permute-done.35
  251.8 3.3 collective-permute-done.34
  257.2 4.6 collective-permute-done.57
  262.7 5.4 %collective-permute-done.58 = bf16[48,768]{1,0:T(8,128)(2,1)S(1)} collective-permute-done((bf16[48,768]{1,0:T(8,128)(2,1)S(1)}, bf16[48,768]{1,0:T(8,128)(2,1)S(1)}, u32[]{:S(2)}, u32[]{:S(2)}) %collective-permute-start.58) | collective-permute-done | bytes 73760 | tf_op jit(solution)/shard_map/ppermute | solution.py:52
  268.9 5.4 %collective-permute-done.59 = bf16[48,768]{1,0:T(8,128)(2,1)S(1)} collective-permute-done((bf16[48,768]{1,0:T(8,128)(2,1)S(1)}, bf16[48,768]{1,0:T(8,128)(2,1)S(1)}, u32[]{:S(2)}, u32[]{:S(2)}) %collective-permute-start.59) | collective-permute-done | bytes 73760 | tf_op jit(solution)/shard_map/ppermute | solution.py:52
  275.2 5.4 %collective-permute-done.60 = bf16[48,768]{1,0:T(8,128)(2,1)S(1)} collective-permute-done((bf16[48,768]{1,0:T(8,128)(2,1)S(1)}, bf16[48,768]{1,0:T(8,128)(2,1)S(1)}, u32[]{:S(2)}, u32[]{:S(2)}) %collective-permute-start.60) | collective-permute-done | bytes 73760 | tf_op jit(solution)/shard_map/ppermute | solution.py:52
  281.3 5.4 %collective-permute-done.61 = bf16[48,768]{1,0:T(8,128)(2,1)S(1)} collective-permute-done((bf16[48,768]{1,0:T(8,128)(2,1)S(1)}, bf16[48,768]{1,0:T(8,128)(2,1)S(1)}, u32[]{:S(2)}, u32[]{:S(2)}) %collective-permute-start.61) | collective-permute-done | bytes 73760 | tf_op jit(solution)/shard_map/ppermute | solution.py:52
  287.9 5.2 %collective-permute-done.62 = bf16[48,768]{1,0:T(8,128)(2,1)S(1)} collective-permute-done((bf16[48,768]{1,0:T(8,128)(2,1)S(1)}, bf16[48,768]{1,0:T(8,128)(2,1)S(1)}, u32[]{:S(2)}, u32[]{:S(2)}) %collective-permute-start.62) | collective-permute-done | bytes 73760 | tf_op jit(solution)/shard_map/ppermute | solution.py:52
  294.5 3.0 collective-permute-done.63
  298.7 3.5 collective-permute-done.64
  303.4 3.1 collective-permute-done.65
  307.8 3.1 collective-permute-done.66
  313.6 19.9 %collective-permute-done.43 = bf16[768,576]{0,1:T(8,128)(2,1)S(1)} collective-permute-done((bf16[768,576]{0,1:T(8,128)(2,1)S(1)}, bf16[768,576]{0,1:T(8,128)(2,1)S(1)}, u32[]{:S(2)}, u32[]{:S(2)}) %collective-permute-start.43) | collective-permute-done | bytes 884768 | tf_op jit(solution)/shard_map/ppermute | solution.py:52
  337.0 7.3 %collective-permute-done.44 = bf16[192,576]{0,1:T(8,128)(2,1)S(1)} collective-permute-done((bf16[192,576]{0,1:T(8,128)(2,1)S(1)}, bf16[192,576]{0,1:T(8,128)(2,1)S(1)}, u32[]{:S(2)}, u32[]{:S(2)}) %collective-permute-start.44) | collective-permute-done | bytes 221216 | tf_op jit(solution)/shard_map/ppermute | solution.py:52
  344.6 9.8 %collective-permute-done.45 = bf16[192,576]{0,1:T(8,128)(2,1)S(1)} collective-permute-done((bf16[192,576]{0,1:T(8,128)(2,1)S(1)}, bf16[192,576]{0,1:T(8,128)(2,1)S(1)}, u32[]{:S(2)}, u32[]{:S(2)}) %collective-permute-start.45) | collective-permute-done | bytes 221216 | tf_op jit(solution)/shard_map/ppermute | solution.py:52
  354.7 4.1 collective-permute-done.82
  359.3 14.8 %collective-permute-done.69 = bf16[768,768]{1,0:T(8,128)(2,1)S(1)} collective-permute-done((bf16[768,768]{1,0:T(8,128)(2,1)S(1)}, bf16[768,768]{1,0:T(8,128)(2,1)S(1)}, u32[]{:S(2)}, u32[]{:S(2)}) %collective-permute-start.69) | collective-permute-done | bytes 1179680 | tf_op jit(solution)/shard_map/ppermute | solution.py:52
  375.5 4.2 collective-permute-start.84
  379.7 6.5 %collective-permute-done.70 = bf16[192,768]{1,0:T(8,128)(2,1)S(1)} collective-permute-done((bf16[192,768]{1,0:T(8,128)(2,1)S(1)}, bf16[192,768]{1,0:T(8,128)(2,1)S(1)}, u32[]{:S(2)}, u32[]{:S(2)}) %collective-permute-start.70) | collective-permute-done | bytes 294944 | tf_op jit(solution)/shard_map/ppermute | solution.py:52
  388.4 4.1 collective-permute-done.47
  393.7 5.1 collective-permute-done.84
  399.0 6.2 %collective-permute-done.71 = bf16[192,768]{1,0:T(8,128)(2,1)S(1)} collective-permute-done((bf16[192,768]{1,0:T(8,128)(2,1)S(1)}, bf16[192,768]{1,0:T(8,128)(2,1)S(1)}, u32[]{:S(2)}, u32[]{:S(2)}) %collective-permute-start.71) | collective-permute-done | bytes 294944 | tf_op jit(solution)/shard_map/ppermute | solution.py:52
  405.4 6.1 %collective-permute-done.48 = bf16[192,576]{0,1:T(8,128)(2,1)S(1)} collective-permute-done((bf16[192,576]{0,1:T(8,128)(2,1)S(1)}, bf16[192,576]{0,1:T(8,128)(2,1)S(1)}, u32[]{:S(2)}, u32[]{:S(2)}) %collective-permute-start.48) | collective-permute-done | bytes 221216 | tf_op jit(solution)/shard_map/ppermute | solution.py:52
  412.7 5.1 collective-permute-done.85
  417.9 6.2 %collective-permute-done.72 = bf16[192,768]{1,0:T(8,128)(2,1)S(1)} collective-permute-done((bf16[192,768]{1,0:T(8,128)(2,1)S(1)}, bf16[192,768]{1,0:T(8,128)(2,1)S(1)}, u32[]{:S(2)}, u32[]{:S(2)}) %collective-permute-start.72) | collective-permute-done | bytes 294944 | tf_op jit(solution)/shard_map/ppermute | solution.py:52
  425.0 5.4 %collective-permute-done.49 = bf16[192,576]{0,1:T(8,128)(2,1)S(1)} collective-permute-done((bf16[192,576]{0,1:T(8,128)(2,1)S(1)}, bf16[192,576]{0,1:T(8,128)(2,1)S(1)}, u32[]{:S(2)}, u32[]{:S(2)}) %collective-permute-start.49) | collective-permute-done | bytes 221216 | tf_op jit(solution)/shard_map/ppermute | solution.py:52
  431.6 5.2 %collective-permute-done.86 = bf16[192,768]{1,0:T(8,128)(2,1)} collective-permute-done((bf16[192,768]{1,0:T(8,128)(2,1)S(1)}, bf16[192,768]{1,0:T(8,128)(2,1)}, u32[]{:S(2)}, u32[]{:S(2)}) %collective-permute-start.86) | collective-permute-done | bytes 294944 | tf_op jit(solution)/shard_map/ppermute | solution.py:52
  439.6 3.5 collective-permute-done.73
  444.1 3.0 concatenate.98
  447.0 2.5 collective-permute-done.87
  449.9 5.6 %collective-permute-done.74 = bf16[192,768]{1,0:T(8,128)(2,1)} collective-permute-done((bf16[192,768]{1,0:T(8,128)(2,1)}, bf16[192,768]{1,0:T(8,128)(2,1)}, u32[]{:S(2)}, u32[]{:S(2)}) %collective-permute-start.74) | collective-permute-done | bytes 294944 | tf_op jit(solution)/shard_map/ppermute | solution.py:52
  460.3 4.3 collective-permute-done.75
  470.1 5.0 collective-permute-done.76
  476.5 10.1 %collective-permute-done.77 = bf16[192,768]{1,0:T(8,128)(2,1)S(1)} collective-permute-done((bf16[192,768]{1,0:T(8,128)(2,1)}, bf16[192,768]{1,0:T(8,128)(2,1)S(1)}, u32[]{:S(2)}, u32[]{:S(2)}) %collective-permute-start.77) | collective-permute-done | bytes 294944 | tf_op jit(solution)/shard_map/ppermute | solution.py:52
  (602 shorter events, 184.1 us)
Async XLA Ops:
  2.9 18.6 %collective-permute-start.4 = (s32[3,512]{1,0:T(4,128)S(1)}, s32[3,512]{1,0:T(4,128)S(1)}, u32[]{:S(2)}, u32[]{:S(2)}) collective-permute-start(s32[3,512]{1,0:T(4,128)S(1)} %concatenate.80), channel_id=1, source_target_pairs={{0,4},{1,5},{2,6},{3,7},{4,0},{5,1},{6,2},{7,3},{8,12},{9,13},{10,... | collective-permute-start | bytes 18440 | tf_op jit(solution)/shard_map/ppermute | solution.py:52
  8.3 28.6 %collective-permute-start.11 = (bf16[96,768]{1,0:T(8,128)(2,1)}, bf16[96,768]{1,0:T(8,128)(2,1)}, u32[]{:S(2)}, u32[]{:S(2)}) collective-permute-start(bf16[96,768]{1,0:T(8,128)(2,1)} %constant_dynamic-slice_fusion.7), channel_id=1, source_target_pairs={{0,2},{1,3},{2,0},{3,1},{4,6},{5,7},{6,4},{7,5},{8,10},{9,11},{10,... | collective-permute-start | bytes 442376 | tf_op jit(solution)/shard_map/ppermute | solution.py:52
  10.9 15.6 %collective-permute-start = (bf16[128,768]{1,0:T(8,128)(2,1)}, bf16[128,768]{1,0:T(8,128)(2,1)S(1)}, u32[]{:S(2)}, u32[]{:S(2)}) collective-permute-start(bf16[128,768]{1,0:T(8,128)(2,1)} %get-tuple-element.87), channel_id=1, source_target_pairs={{0,0},{1,4},{2,2},{3,6},{4,1},{5,5},{6,3},{7,7},{8,8},{9,12},{10,1... | collective-permute-start | bytes 589832 | tf_op jit(solution)/shard_map/ppermute | solution.py:52
  12.4 15.6 %collective-permute-start.3 = (bf16[128,768]{1,0:T(8,128)(2,1)}, bf16[128,768]{1,0:T(8,128)(2,1)S(1)}, u32[]{:S(2)}, u32[]{:S(2)}) collective-permute-start(bf16[128,768]{1,0:T(8,128)(2,1)} %get-tuple-element.88), channel_id=1, source_target_pairs={{0,6},{1,2},{2,4},{3,0},{4,7},{5,3},{6,5},{7,1},{8,14},{9,10},{10,... | collective-permute-start | bytes 589832 | tf_op jit(solution)/shard_map/ppermute | solution.py:52
  13.7 16.1 %collective-permute-start.1 = (bf16[128,768]{1,0:T(8,128)(2,1)}, bf16[128,768]{1,0:T(8,128)(2,1)S(1)}, u32[]{:S(2)}, u32[]{:S(2)}) collective-permute-start(bf16[128,768]{1,0:T(8,128)(2,1)} %get-tuple-element.89), channel_id=1, source_target_pairs={{0,4},{1,0},{2,6},{3,2},{4,5},{5,1},{6,7},{7,3},{8,12},{9,8},{10,1... | collective-permute-start | bytes 589832 | tf_op jit(solution)/shard_map/ppermute | solution.py:52
  26.5 11.8 %collective-permute-start.31 = (bf16[128,768]{1,0:T(8,128)(2,1)}, bf16[128,768]{1,0:T(8,128)(2,1)S(1)}, u32[]{:S(2)}, u32[]{:S(2)}) collective-permute-start(bf16[128,768]{1,0:T(8,128)(2,1)} %get-tuple-element.75), channel_id=1, source_target_pairs={{0,6},{1,2},{2,4},{3,0},{4,7},{5,3},{6,5},{7,1},{8,14},{9,10},{10,... | collective-permute-start | bytes 589832 | tf_op jit(solution)/shard_map/ppermute | solution.py:52
  28.1 11.3 %collective-permute-start.28 = (bf16[128,768]{1,0:T(8,128)(2,1)}, bf16[128,768]{1,0:T(8,128)(2,1)S(1)}, u32[]{:S(2)}, u32[]{:S(2)}) collective-permute-start(bf16[128,768]{1,0:T(8,128)(2,1)} %get-tuple-element.76), channel_id=1, source_target_pairs={{0,0},{1,4},{2,2},{3,6},{4,1},{5,5},{6,3},{7,7},{8,8},{9,12},{10,1... | collective-permute-start | bytes 589832 | tf_op jit(solution)/shard_map/ppermute | solution.py:52
  29.8 10.6 %collective-permute-start.29 = (bf16[128,768]{1,0:T(8,128)(2,1)}, bf16[128,768]{1,0:T(8,128)(2,1)S(1)}, u32[]{:S(2)}, u32[]{:S(2)}) collective-permute-start(bf16[128,768]{1,0:T(8,128)(2,1)} %get-tuple-element.78), channel_id=1, source_target_pairs={{0,4},{1,0},{2,6},{3,2},{4,5},{5,1},{6,7},{7,3},{8,12},{9,8},{10,1... | collective-permute-start | bytes 589832 | tf_op jit(solution)/shard_map/ppermute | solution.py:52
  31.3 13.3 %collective-permute-start.8 = (bf16[384,576]{0,1:T(8,128)(2,1)}, bf16[384,576]{0,1:T(8,128)(2,1)S(1)}, u32[]{:S(2)}, u32[]{:S(2)}) collective-permute-start(bf16[384,576]{0,1:T(8,128)(2,1)} %constant_dynamic-slice_fusion.8), channel_id=1, source_target_pairs={{0,2},{1,3},{2,0},{3,1},{4,6},{5,7},{6,4},{7,5},{8,10},{9,11},{10,... | collective-permute-start | bytes 1327112 | tf_op jit(solution)/shard_map/ppermute | solution.py:52
  37.3 44.0 %collective-permute-start.18 = (bf16[384,768]{1,0:T(8,128)(2,1)S(1)}, bf16[384,768]{1,0:T(8,128)(2,1)S(1)}, u32[]{:S(2)}, u32[]{:S(2)}) collective-permute-start(bf16[384,768]{1,0:T(8,128)(2,1)S(1)} %copy-done.75), channel_id=1, source_target_pairs={{0,2},{1,3},{2,0},{3,1},{4,6},{5,7},{6,4},{7,5},{8,10},{9,11},{10,... | collective-permute-start | bytes 1769480 | tf_op jit(solution)/shard_map/ppermute | solution.py:52
  38.3 43.2 %collective-permute-start.20 = (bf16[384,768]{1,0:T(8,128)(2,1)S(1)}, bf16[384,768]{1,0:T(8,128)(2,1)S(1)}, u32[]{:S(2)}, u32[]{:S(2)}) collective-permute-start(bf16[384,768]{1,0:T(8,128)(2,1)S(1)} %copy-done.74), channel_id=1, source_target_pairs={{0,2},{1,3},{2,0},{3,1},{4,6},{5,7},{6,4},{7,5},{8,10},{9,11},{10,... | collective-permute-start | bytes 1769480 | tf_op jit(solution)/shard_map/ppermute | solution.py:52
  39.4 33.6 %collective-permute-start.30 = (bf16[128,768]{1,0:T(8,128)(2,1)S(1)}, bf16[128,768]{1,0:T(8,128)(2,1)S(1)}, u32[]{:S(2)}, u32[]{:S(2)}) collective-permute-start(bf16[128,768]{1,0:T(8,128)(2,1)S(1)} %copy-done.88), channel_id=1, source_target_pairs={{0,2},{1,6},{2,0},{3,4},{4,3},{5,7},{6,1},{7,5},{8,10},{9,14},{10,... | collective-permute-start | bytes 589832 | tf_op jit(solution)/shard_map/ppermute | solution.py:52
  40.4 44.0 %collective-permute-start.5 = (bf16[768,576]{0,1:T(8,128)(2,1)S(1)}, bf16[768,576]{0,1:T(8,128)(2,1)S(1)}, u32[]{:S(2)}, u32[]{:S(2)}) collective-permute-start(bf16[768,576]{0,1:T(8,128)(2,1)S(1)} %copy-done.25), channel_id=1, source_target_pairs={{0,1},{1,0},{2,3},{3,2},{4,5},{5,4},{6,7},{7,6},{8,9},{9,8},{10,11... | collective-permute-start | bytes 2654216 | tf_op jit(solution)/shard_map/ppermute | solution.py:52
  44.7 38.5 %collective-permute-start.9 = (bf16[384,576]{0,1:T(8,128)(2,1)S(1)}, bf16[384,576]{0,1:T(8,128)(2,1)S(1)}, u32[]{:S(2)}, u32[]{:S(2)}) collective-permute-start(bf16[384,576]{0,1:T(8,128)(2,1)S(1)} %collective-permute-done.8), channel_id=1, source_target_pairs={{0,8},{1,9},{2,10},{3,11},{4,12},{5,13},{6,14},{7,15},{8,0},{9,1},... | collective-permute-start | bytes 1327112 | tf_op jit(solution)/shard_map/ppermute | solution.py:52
  79.5 30.9 %collective-permute-start.10 = (f32[3]{0:T(128)S(1)}, f32[3]{0:T(128)S(1)}, u32[]{:S(2)}, u32[]{:S(2)}) collective-permute-start(f32[3]{0:T(128)S(1)} %copy-done.113), channel_id=1, source_target_pairs={{0,2},{1,3},{2,0},{3,1},{4,6},{5,7},{6,4},{7,5},{8,10},{9,11},{10,... | collective-permute-start | bytes 44 | tf_op jit(solution)/shard_map/ppermute | solution.py:52
  81.4 31.3 %collective-permute-start.6 = (f32[3]{0:T(128)S(1)}, f32[3]{0:T(128)S(1)}, u32[]{:S(2)}, u32[]{:S(2)}) collective-permute-start(f32[3]{0:T(128)S(1)} %copy-done.113), channel_id=1, source_target_pairs={{0,1},{1,0},{2,3},{3,2},{4,5},{5,4},{6,7},{7,6},{8,9},{9,8},{10,11... | collective-permute-start | bytes 44 | tf_op jit(solution)/shard_map/ppermute | solution.py:52
  81.5 16.2 %collective-permute-start.19 = (bf16[384,768]{1,0:T(8,128)(2,1)S(1)}, bf16[384,768]{1,0:T(8,128)(2,1)S(1)}, u32[]{:S(2)}, u32[]{:S(2)}) collective-permute-start(bf16[384,768]{1,0:T(8,128)(2,1)S(1)} %collective-permute-done.18), channel_id=1, source_target_pairs={{0,8},{1,9},{2,10},{3,11},{4,12},{5,13},{6,14},{7,15},{8,0},{9,1},... | collective-permute-start | bytes 1769480 | tf_op jit(solution)/shard_map/ppermute | solution.py:52
  83.1 26.7 %collective-permute-start.21 = (bf16[384,768]{1,0:T(8,128)(2,1)S(1)}, bf16[384,768]{1,0:T(8,128)(2,1)S(1)}, u32[]{:S(2)}, u32[]{:S(2)}) collective-permute-start(bf16[384,768]{1,0:T(8,128)(2,1)S(1)} %collective-permute-done.20), channel_id=1, source_target_pairs={{0,8},{1,9},{2,10},{3,11},{4,12},{5,13},{6,14},{7,15},{8,0},{9,1},... | collective-permute-start | bytes 1769480 | tf_op jit(solution)/shard_map/ppermute | solution.py:52
  84.5 26.4 %collective-permute-start.13 = (bf16[768,576]{0,1:T(8,128)(2,1)S(1)}, bf16[768,576]{0,1:T(8,128)(2,1)S(1)}, u32[]{:S(2)}, u32[]{:S(2)}) collective-permute-start(bf16[768,576]{0,1:T(8,128)(2,1)S(1)} %maximum_select_fusion.3), channel_id=1, source_target_pairs={{0,1},{1,0},{2,3},{3,2},{4,5},{5,4},{6,7},{7,6},{8,9},{9,8},{10,11... | collective-permute-start | bytes 2654216 | tf_op jit(solution)/shard_map/ppermute | solution.py:52
  97.7 21.4 %collective-permute-start.7 = (bf16[192,768]{1,0:T(8,128)(2,1)S(1)}, bf16[192,768]{1,0:T(8,128)(2,1)S(1)}, u32[]{:S(2)}, u32[]{:S(2)}) collective-permute-start(bf16[192,768]{1,0:T(8,128)(2,1)S(1)} %copy-done.18), channel_id=1, source_target_pairs={{0,1},{1,0},{2,3},{3,2},{4,5},{5,4},{6,7},{7,6},{8,9},{9,8},{10,11... | collective-permute-start | bytes 884744 | tf_op jit(solution)/shard_map/ppermute | solution.py:52
  109.9 25.7 %collective-permute-start.17 = (bf16[768,768]{1,0:T(8,128)(2,1)S(1)}, bf16[768,768]{1,0:T(8,128)(2,1)}, u32[]{:S(2)}, u32[]{:S(2)}) collective-permute-start(bf16[768,768]{1,0:T(8,128)(2,1)S(1)} %copy-done.23), channel_id=1, source_target_pairs={{0,1},{1,0},{2,3},{3,2},{4,5},{5,4},{6,7},{7,6},{8,9},{9,8},{10,11... | collective-permute-start | bytes 3538952 | tf_op jit(solution)/shard_map/ppermute | solution.py:52
  110.4 15.2 %collective-permute-start.16 = (bf16[768,768]{1,0:T(8,128)(2,1)S(1)}, bf16[768,768]{1,0:T(8,128)(2,1)}, u32[]{:S(2)}, u32[]{:S(2)}) collective-permute-start(bf16[768,768]{1,0:T(8,128)(2,1)S(1)} %copy-done.21), channel_id=1, source_target_pairs={{0,1},{1,0},{2,3},{3,2},{4,5},{5,4},{6,7},{7,6},{8,9},{9,8},{10,11... | collective-permute-start | bytes 3538952 | tf_op jit(solution)/shard_map/ppermute | solution.py:52
  112.9 39.3 %collective-permute-start.23 = (bf16[768,768]{1,0:T(8,128)(2,1)S(1)}, bf16[768,768]{1,0:T(8,128)(2,1)}, u32[]{:S(2)}, u32[]{:S(2)}) collective-permute-start(bf16[768,768]{1,0:T(8,128)(2,1)S(1)} %maximum_select_fusion.1), channel_id=1, source_target_pairs={{0,1},{1,0},{2,3},{3,2},{4,5},{5,4},{6,7},{7,6},{8,9},{9,8},{10,11... | collective-permute-start | bytes 3538952 | tf_op jit(solution)/shard_map/ppermute | solution.py:52
  119.1 30.3 %collective-permute-start.22 = (bf16[768,768]{1,0:T(8,128)(2,1)S(1)}, bf16[768,768]{1,0:T(8,128)(2,1)S(1)}, u32[]{:S(2)}, u32[]{:S(2)}) collective-permute-start(bf16[768,768]{1,0:T(8,128)(2,1)S(1)} %maximum_select_fusion), channel_id=1, source_target_pairs={{0,1},{1,0},{2,3},{3,2},{4,5},{5,4},{6,7},{7,6},{8,9},{9,8},{10,11... | collective-permute-start | bytes 3538952 | tf_op jit(solution)/shard_map/ppermute | solution.py:52
  201.6 37.2 %collective-permute-start.26 = (bf16[128,768]{1,0:T(8,128)(2,1)S(1)}, bf16[128,768]{1,0:T(8,128)(2,1)S(1)}, u32[]{:S(2)}, u32[]{:S(2)}) collective-permute-start(bf16[128,768]{1,0:T(8,128)(2,1)S(1)} %get-tuple-element.84), channel_id=1, source_target_pairs={{0,2},{1,6},{2,0},{3,4},{4,3},{5,7},{6,1},{7,5},{8,10},{9,14},{10,... | collective-permute-start | bytes 589832 | tf_op jit(solution)/shard_map/ppermute | solution.py:52
  202.8 36.0 %collective-permute-start.25 = (bf16[128,768]{1,0:T(8,128)(2,1)S(1)}, bf16[128,768]{1,0:T(8,128)(2,1)S(1)}, u32[]{:S(2)}, u32[]{:S(2)}) collective-permute-start(bf16[128,768]{1,0:T(8,128)(2,1)S(1)} %get-tuple-element.85), channel_id=1, source_target_pairs={{0,1},{1,5},{2,3},{3,7},{4,0},{5,4},{6,2},{7,6},{8,9},{9,13},{10,1... | collective-permute-start | bytes 589832 | tf_op jit(solution)/shard_map/ppermute | solution.py:52
  203.0 37.1 %collective-permute-start.24 = (bf16[128,768]{1,0:T(8,128)(2,1)S(1)}, bf16[128,768]{1,0:T(8,128)(2,1)S(1)}, u32[]{:S(2)}, u32[]{:S(2)}) collective-permute-start(bf16[128,768]{1,0:T(8,128)(2,1)S(1)} %get-tuple-element.86), channel_id=1, source_target_pairs={{0,0},{1,4},{2,2},{3,6},{4,1},{5,5},{6,3},{7,7},{8,8},{9,12},{10,1... | collective-permute-start | bytes 589832 | tf_op jit(solution)/shard_map/ppermute | solution.py:52
  238.8 42.5 %collective-permute-start.67 = (bf16[768,768]{1,0:T(8,128)(2,1)S(1)}, bf16[768,768]{1,0:T(8,128)(2,1)S(1)}, u32[]{:S(2)}, u32[]{:S(2)}) collective-permute-start(bf16[768,768]{1,0:T(8,128)(2,1)S(1)} %copy-done.108), channel_id=1, source_target_pairs={{0,1},{1,0},{2,3},{3,2},{4,5},{5,4},{6,7},{7,6},{8,9},{9,8},{10,11... | collective-permute-start | bytes 3538952 | tf_op jit(solution)/shard_map/ppermute | solution.py:52
  238.9 12.9 %collective-permute-start.35 = (bf16[128,768]{1,0:T(8,128)(2,1)S(1)}, bf16[128,768]{1,0:T(8,128)(2,1)S(1)}, u32[]{:S(2)}, u32[]{:S(2)}) collective-permute-start(bf16[128,768]{1,0:T(8,128)(2,1)S(1)} %get-tuple-element.71), channel_id=1, source_target_pairs={{0,3},{1,7},{2,1},{3,5},{4,2},{5,6},{6,0},{7,4},{8,11},{9,15},{10,... | collective-permute-start | bytes 589832 | tf_op jit(solution)/shard_map/ppermute | solution.py:52
  240.1 14.9 %collective-permute-start.34 = (bf16[128,768]{1,0:T(8,128)(2,1)S(1)}, bf16[128,768]{1,0:T(8,128)(2,1)S(1)}, u32[]{:S(2)}, u32[]{:S(2)}) collective-permute-start(bf16[128,768]{1,0:T(8,128)(2,1)S(1)} %get-tuple-element.72), channel_id=1, source_target_pairs={{0,2},{1,6},{2,0},{3,4},{4,3},{5,7},{6,1},{7,5},{8,10},{9,14},{10,... | collective-permute-start | bytes 589832 | tf_op jit(solution)/shard_map/ppermute | solution.py:52
  241.1 14.3 %collective-permute-start.33 = (bf16[128,768]{1,0:T(8,128)(2,1)S(1)}, bf16[128,768]{1,0:T(8,128)(2,1)S(1)}, u32[]{:S(2)}, u32[]{:S(2)}) collective-permute-start(bf16[128,768]{1,0:T(8,128)(2,1)S(1)} %get-tuple-element.73), channel_id=1, source_target_pairs={{0,1},{1,5},{2,3},{3,7},{4,0},{5,4},{6,2},{7,6},{8,9},{9,13},{10,1... | collective-permute-start | bytes 589832 | tf_op jit(solution)/shard_map/ppermute | solution.py:52
  251.8 102.9 %collective-permute-start.80 = (bf16[768,768]{1,0:T(8,128)(2,1)S(1)}, bf16[768,768]{1,0:T(8,128)(2,1)S(1)}, u32[]{:S(2)}, u32[]{:S(2)}) collective-permute-start(bf16[768,768]{1,0:T(8,128)(2,1)S(1)} %copy-done.106), channel_id=1, source_target_pairs={{0,1},{1,0},{2,3},{3,2},{4,5},{5,4},{6,7},{7,6},{8,9},{9,8},{10,11... | collective-permute-start | bytes 3538952 | tf_op jit(solution)/shard_map/ppermute | solution.py:52
  255.0 79.0 %collective-permute-start.68 = (bf16[768,768]{1,0:T(8,128)(2,1)S(1)}, bf16[768,768]{1,0:T(8,128)(2,1)S(1)}, u32[]{:S(2)}, u32[]{:S(2)}) collective-permute-start(bf16[768,768]{1,0:T(8,128)(2,1)S(1)} %convolution_convert_fusion.4), channel_id=1, source_target_pairs={{0,1},{1,0},{2,3},{3,2},{4,5},{5,4},{6,7},{7,6},{8,9},{9,8},{10,11... | collective-permute-start | bytes 3538952 | tf_op jit(solution)/shard_map/ppermute | solution.py:52
  255.4 32.4 %collective-permute-start.42 = (bf16[768,576]{0,1:T(8,128)(2,1)S(1)}, bf16[768,576]{0,1:T(8,128)(2,1)S(1)}, u32[]{:S(2)}, u32[]{:S(2)}) collective-permute-start(bf16[768,576]{0,1:T(8,128)(2,1)S(1)} %convolution_convert_fusion.8), channel_id=1, source_target_pairs={{0,1},{1,0},{2,3},{3,2},{4,5},{5,4},{6,7},{7,6},{8,9},{9,8},{10,11... | collective-permute-start | bytes 2654216 | tf_op jit(solution)/shard_map/ppermute | solution.py:52
  281.3 31.0 %collective-permute-start.81 = (bf16[768,768]{1,0:T(8,128)(2,1)S(1)}, bf16[768,768]{1,0:T(8,128)(2,1)S(1)}, u32[]{:S(2)}, u32[]{:S(2)}) collective-permute-start(bf16[768,768]{1,0:T(8,128)(2,1)S(1)} %copy-done.107), channel_id=1, source_target_pairs={{0,1},{1,0},{2,3},{3,2},{4,5},{5,4},{6,7},{7,6},{8,9},{9,8},{10,11... | collective-permute-start | bytes 3538952 | tf_op jit(solution)/shard_map/ppermute | solution.py:52
  287.8 25.8 %collective-permute-start.41 = (bf16[768,576]{0,1:T(8,128)(2,1)S(1)}, bf16[768,576]{0,1:T(8,128)(2,1)S(1)}, u32[]{:S(2)}, u32[]{:S(2)}) collective-permute-start(bf16[768,576]{0,1:T(8,128)(2,1)S(1)} %convolution_convert_fusion.10), channel_id=1, source_target_pairs={{0,1},{1,0},{2,3},{3,2},{4,5},{5,4},{6,7},{7,6},{8,9},{9,8},{10,11... | collective-permute-start | bytes 2654216 | tf_op jit(solution)/shard_map/ppermute | solution.py:52
  310.9 22.6 %collective-permute-start.43 = (bf16[768,576]{0,1:T(8,128)(2,1)S(1)}, bf16[768,576]{0,1:T(8,128)(2,1)S(1)}, u32[]{:S(2)}, u32[]{:S(2)}) collective-permute-start(bf16[768,576]{0,1:T(8,128)(2,1)S(1)} %add_convert_fusion.7), channel_id=1, source_target_pairs={{0,2},{1,3},{2,0},{3,1},{4,6},{5,7},{6,4},{7,5},{8,10},{9,11},{10,... | collective-permute-start | bytes 2654216 | tf_op jit(solution)/shard_map/ppermute | solution.py:52
  312.7 46.1 %collective-permute-start.82 = (bf16[768,768]{1,0:T(8,128)(2,1)S(1)}, bf16[768,768]{1,0:T(8,128)(2,1)S(1)}, u32[]{:S(2)}, u32[]{:S(2)}) collective-permute-start(bf16[768,768]{1,0:T(8,128)(2,1)S(1)} %add_convert_fusion.1), channel_id=1, source_target_pairs={{0,2},{1,3},{2,0},{3,1},{4,6},{5,7},{6,4},{7,5},{8,10},{9,11},{10,... | collective-permute-start | bytes 3538952 | tf_op jit(solution)/shard_map/ppermute | solution.py:52
  334.0 10.4 %collective-permute-start.44 = (bf16[192,576]{0,1:T(8,128)(2,1)S(1)}, bf16[192,576]{0,1:T(8,128)(2,1)S(1)}, u32[]{:S(2)}, u32[]{:S(2)}) collective-permute-start(bf16[192,576]{0,1:T(8,128)(2,1)S(1)} %constant_dynamic-slice_fusion.3), channel_id=1, source_target_pairs={{0,8},{1,9},{2,10},{3,11},{4,12},{5,13},{6,14},{7,15},{8,16},{9,17... | collective-permute-start | bytes 663560 | tf_op jit(solution)/shard_map/ppermute | solution.py:52
  334.9 39.1 %collective-permute-start.69 = (bf16[768,768]{1,0:T(8,128)(2,1)S(1)}, bf16[768,768]{1,0:T(8,128)(2,1)S(1)}, u32[]{:S(2)}, u32[]{:S(2)}) collective-permute-start(bf16[768,768]{1,0:T(8,128)(2,1)S(1)} %add_convert_fusion.4), channel_id=1, source_target_pairs={{0,2},{1,3},{2,0},{3,1},{4,6},{5,7},{6,4},{7,5},{8,10},{9,11},{10,... | collective-permute-start | bytes 3538952 | tf_op jit(solution)/shard_map/ppermute | solution.py:52
  354.6 19.9 %collective-permute-start.46 = (bf16[192,576]{0,1:T(8,128)(2,1)S(1)}, bf16[192,576]{0,1:T(8,128)(2,1)S(1)}, u32[]{:S(2)}, u32[]{:S(2)}) collective-permute-start(bf16[192,576]{0,1:T(8,128)(2,1)S(1)} %add_convert_fusion.18), channel_id=1, source_target_pairs={{0,8},{1,9},{2,10},{3,11},{4,12},{5,13},{6,14},{7,15},{8,16},{9,17... | collective-permute-start | bytes 663560 | tf_op jit(solution)/shard_map/ppermute | solution.py:52
  359.2 16.1 %collective-permute-start.83 = (bf16[192,768]{1,0:T(8,128)(2,1)S(1)}, bf16[192,768]{1,0:T(8,128)(2,1)S(1)}, u32[]{:S(2)}, u32[]{:S(2)}) collective-permute-start(bf16[192,768]{1,0:T(8,128)(2,1)S(1)} %constant_dynamic-slice_fusion), channel_id=1, source_target_pairs={{0,8},{1,9},{2,10},{3,11},{4,12},{5,13},{6,14},{7,15},{8,16},{9,17... | collective-permute-start | bytes 884744 | tf_op jit(solution)/shard_map/ppermute | solution.py:52
  374.4 11.8 %collective-permute-start.70 = (bf16[192,768]{1,0:T(8,128)(2,1)S(1)}, bf16[192,768]{1,0:T(8,128)(2,1)S(1)}, u32[]{:S(2)}, u32[]{:S(2)}) collective-permute-start(bf16[192,768]{1,0:T(8,128)(2,1)S(1)} %constant_dynamic-slice_fusion.1), channel_id=1, source_target_pairs={{0,8},{1,9},{2,10},{3,11},{4,12},{5,13},{6,14},{7,15},{8,16},{9,17... | collective-permute-start | bytes 884744 | tf_op jit(solution)/shard_map/ppermute | solution.py:52
  374.6 17.9 %collective-permute-start.47 = (bf16[192,576]{0,1:T(8,128)(2,1)S(1)}, bf16[192,576]{0,1:T(8,128)(2,1)S(1)}, u32[]{:S(2)}, u32[]{:S(2)}) collective-permute-start(bf16[192,576]{0,1:T(8,128)(2,1)S(1)} %add_convert_fusion.17), channel_id=1, source_target_pairs={{0,8},{1,9},{2,10},{3,11},{4,12},{5,13},{6,14},{7,15},{8,16},{9,17... | collective-permute-start | bytes 663560 | tf_op jit(solution)/shard_map/ppermute | solution.py:52
  375.5 23.4 %collective-permute-start.84 = (bf16[192,768]{1,0:T(8,128)(2,1)S(1)}, bf16[192,768]{1,0:T(8,128)(2,1)S(1)}, u32[]{:S(2)}, u32[]{:S(2)}) collective-permute-start(bf16[192,768]{1,0:T(8,128)(2,1)S(1)} %add_convert_fusion.13), channel_id=1, source_target_pairs={{0,8},{1,9},{2,10},{3,11},{4,12},{5,13},{6,14},{7,15},{8,16},{9,17... | collective-permute-start | bytes 884744 | tf_op jit(solution)/shard_map/ppermute | solution.py:52
  386.3 18.9 %collective-permute-start.71 = (bf16[192,768]{1,0:T(8,128)(2,1)S(1)}, bf16[192,768]{1,0:T(8,128)(2,1)S(1)}, u32[]{:S(2)}, u32[]{:S(2)}) collective-permute-start(bf16[192,768]{1,0:T(8,128)(2,1)S(1)} %add_convert_fusion.16), channel_id=1, source_target_pairs={{0,8},{1,9},{2,10},{3,11},{4,12},{5,13},{6,14},{7,15},{8,16},{9,17... | collective-permute-start | bytes 884744 | tf_op jit(solution)/shard_map/ppermute | solution.py:52
  387.2 18.1 %collective-permute-start.53 = (bf16[192,576]{0,1:T(8,128)(2,1)S(1)}, bf16[192,576]{0,1:T(8,128)(2,1)S(1)}, u32[]{:S(2)}, u32[]{:S(2)}) collective-permute-start(bf16[192,576]{0,1:T(8,128)(2,1)S(1)} %add_convert_fusion.17), channel_id=1, source_target_pairs={{0,4},{1,5},{2,6},{3,7},{4,0},{5,1},{6,2},{7,3},{8,12},{9,13},{10,... | collective-permute-start | bytes 663560 | tf_op jit(solution)/shard_map/ppermute | solution.py:52
  392.5 31.8 %collective-permute-start.52 = (bf16[192,576]{0,1:T(8,128)(2,1)S(1)}, bf16[192,576]{0,1:T(8,128)(2,1)S(1)}, u32[]{:S(2)}, u32[]{:S(2)}) collective-permute-start(bf16[192,576]{0,1:T(8,128)(2,1)S(1)} %collective-permute-done.47), channel_id=1, source_target_pairs={{0,4},{1,5},{2,6},{3,7},{4,0},{5,1},{6,2},{7,3},{8,12},{9,13},{10,... | collective-permute-start | bytes 663560 | tf_op jit(solution)/shard_map/ppermute | solution.py:52
  393.7 17.7 %collective-permute-start.48 = (bf16[192,576]{0,1:T(8,128)(2,1)S(1)}, bf16[192,576]{0,1:T(8,128)(2,1)S(1)}, u32[]{:S(2)}, u32[]{:S(2)}) collective-permute-start(bf16[192,576]{0,1:T(8,128)(2,1)S(1)} %collective-permute-done.47), channel_id=1, source_target_pairs={{0,8},{1,9},{2,10},{3,11},{4,12},{5,13},{6,14},{7,15},{8,16},{9,17... | collective-permute-start | bytes 663560 | tf_op jit(solution)/shard_map/ppermute | solution.py:52
  398.9 18.9 %collective-permute-start.85 = (bf16[192,768]{1,0:T(8,128)(2,1)S(1)}, bf16[192,768]{1,0:T(8,128)(2,1)S(1)}, u32[]{:S(2)}, u32[]{:S(2)}) collective-permute-start(bf16[192,768]{1,0:T(8,128)(2,1)S(1)} %add_convert_fusion.12), channel_id=1, source_target_pairs={{0,8},{1,9},{2,10},{3,11},{4,12},{5,13},{6,14},{7,15},{8,16},{9,17... | collective-permute-start | bytes 884744 | tf_op jit(solution)/shard_map/ppermute | solution.py:52
  405.2 18.9 %collective-permute-start.72 = (bf16[192,768]{1,0:T(8,128)(2,1)S(1)}, bf16[192,768]{1,0:T(8,128)(2,1)S(1)}, u32[]{:S(2)}, u32[]{:S(2)}) collective-permute-start(bf16[192,768]{1,0:T(8,128)(2,1)S(1)} %add_convert_fusion.15), channel_id=1, source_target_pairs={{0,8},{1,9},{2,10},{3,11},{4,12},{5,13},{6,14},{7,15},{8,16},{9,17... | collective-permute-start | bytes 884744 | tf_op jit(solution)/shard_map/ppermute | solution.py:52
  411.5 25.4 %collective-permute-start.51 = (bf16[192,576]{0,1:T(8,128)(2,1)S(1)}, bf16[192,576]{0,1:T(8,128)(2,1)S(1)}, u32[]{:S(2)}, u32[]{:S(2)}) collective-permute-start(bf16[192,576]{0,1:T(8,128)(2,1)S(1)} %collective-permute-done.48), channel_id=1, source_target_pairs={{0,4},{1,5},{2,6},{3,7},{4,0},{5,1},{6,2},{7,3},{8,12},{9,13},{10,... | collective-permute-start | bytes 663560 | tf_op jit(solution)/shard_map/ppermute | solution.py:52
  412.7 17.7 %collective-permute-start.49 = (bf16[192,576]{0,1:T(8,128)(2,1)S(1)}, bf16[192,576]{0,1:T(8,128)(2,1)S(1)}, u32[]{:S(2)}, u32[]{:S(2)}) collective-permute-start(bf16[192,576]{0,1:T(8,128)(2,1)S(1)} %collective-permute-done.48), channel_id=1, source_target_pairs={{0,8},{1,9},{2,10},{3,11},{4,12},{5,13},{6,14},{7,15},{8,16},{9,17... | collective-permute-start | bytes 663560 | tf_op jit(solution)/shard_map/ppermute | solution.py:52
  417.9 19.0 %collective-permute-start.86 = (bf16[192,768]{1,0:T(8,128)(2,1)S(1)}, bf16[192,768]{1,0:T(8,128)(2,1)}, u32[]{:S(2)}, u32[]{:S(2)}) collective-permute-start(bf16[192,768]{1,0:T(8,128)(2,1)S(1)} %add_convert_fusion.11), channel_id=1, source_target_pairs={{0,8},{1,9},{2,10},{3,11},{4,12},{5,13},{6,14},{7,15},{8,16},{9,17... | collective-permute-start | bytes 884744 | tf_op jit(solution)/shard_map/ppermute | solution.py:52
  424.2 19.0 %collective-permute-start.73 = (bf16[192,768]{1,0:T(8,128)(2,1)S(1)}, bf16[192,768]{1,0:T(8,128)(2,1)}, u32[]{:S(2)}, u32[]{:S(2)}) collective-permute-start(bf16[192,768]{1,0:T(8,128)(2,1)S(1)} %add_convert_fusion.14), channel_id=1, source_target_pairs={{0,8},{1,9},{2,10},{3,11},{4,12},{5,13},{6,14},{7,15},{8,16},{9,17... | collective-permute-start | bytes 884744 | tf_op jit(solution)/shard_map/ppermute | solution.py:52
  430.4 12.8 %collective-permute-start.50 = (bf16[192,576]{0,1:T(8,128)(2,1)S(1)}, bf16[192,576]{0,1:T(8,128)(2,1)S(1)}, u32[]{:S(2)}, u32[]{:S(2)}) collective-permute-start(bf16[192,576]{0,1:T(8,128)(2,1)S(1)} %collective-permute-done.49), channel_id=1, source_target_pairs={{0,4},{1,5},{2,6},{3,7},{4,0},{5,1},{6,2},{7,3},{8,12},{9,13},{10,... | collective-permute-start | bytes 663560 | tf_op jit(solution)/shard_map/ppermute | solution.py:52
  436.8 12.6 %collective-permute-start.87 = (bf16[192,768]{1,0:T(8,128)(2,1)}, bf16[192,768]{1,0:T(8,128)(2,1)}, u32[]{:S(2)}, u32[]{:S(2)}) collective-permute-start(bf16[192,768]{1,0:T(8,128)(2,1)} %collective-permute-done.86), channel_id=1, source_target_pairs={{0,8},{1,9},{2,10},{3,11},{4,12},{5,13},{6,14},{7,15},{8,16},{9,17... | collective-permute-start | bytes 884744 | tf_op jit(solution)/shard_map/ppermute | solution.py:52
  437.6 50.4 %collective-permute-start.79 = (bf16[192,768]{1,0:T(8,128)(2,1)S(1)}, bf16[192,768]{1,0:T(8,128)(2,1)}, u32[]{:S(2)}, u32[]{:S(2)}) collective-permute-start(bf16[192,768]{1,0:T(8,128)(2,1)S(1)} %add_convert_fusion.14), channel_id=1, source_target_pairs={{0,4},{1,5},{2,6},{3,7},{4,0},{5,1},{6,2},{7,3},{8,12},{9,13},{10,... | collective-permute-start | bytes 884744 | tf_op jit(solution)/shard_map/ppermute | solution.py:52
  438.8 61.2 %collective-permute-start.92 = (bf16[192,768]{1,0:T(8,128)(2,1)S(1)}, bf16[192,768]{1,0:T(8,128)(2,1)}, u32[]{:S(2)}, u32[]{:S(2)}) collective-permute-start(bf16[192,768]{1,0:T(8,128)(2,1)S(1)} %add_convert_fusion.11), channel_id=1, source_target_pairs={{0,4},{1,5},{2,6},{3,7},{4,0},{5,1},{6,2},{7,3},{8,12},{9,13},{10,... | collective-permute-start | bytes 884744 | tf_op jit(solution)/shard_map/ppermute | solution.py:52
  443.2 12.3 %collective-permute-start.74 = (bf16[192,768]{1,0:T(8,128)(2,1)}, bf16[192,768]{1,0:T(8,128)(2,1)}, u32[]{:S(2)}, u32[]{:S(2)}) collective-permute-start(bf16[192,768]{1,0:T(8,128)(2,1)} %collective-permute-done.73), channel_id=1, source_target_pairs={{0,8},{1,9},{2,10},{3,11},{4,12},{5,13},{6,14},{7,15},{8,16},{9,17... | collective-permute-start | bytes 884744 | tf_op jit(solution)/shard_map/ppermute | solution.py:52
  464.6 10.5 %collective-permute-start.76 = (bf16[192,768]{1,0:T(8,128)(2,1)}, bf16[192,768]{1,0:T(8,128)(2,1)S(1)}, u32[]{:S(2)}, u32[]{:S(2)}) collective-permute-start(bf16[192,768]{1,0:T(8,128)(2,1)} %collective-permute-done.75), channel_id=1, source_target_pairs={{0,4},{1,5},{2,6},{3,7},{4,0},{5,1},{6,2},{7,3},{8,12},{9,13},{10,... | collective-permute-start | bytes 884744 | tf_op jit(solution)/shard_map/ppermute | solution.py:52
  467.1 20.8 %collective-permute-start.78 = (bf16[192,768]{1,0:T(8,128)(2,1)}, bf16[192,768]{1,0:T(8,128)(2,1)S(1)}, u32[]{:S(2)}, u32[]{:S(2)}) collective-permute-start(bf16[192,768]{1,0:T(8,128)(2,1)} %collective-permute-done.73), channel_id=1, source_target_pairs={{0,4},{1,5},{2,6},{3,7},{4,0},{5,1},{6,2},{7,3},{8,12},{9,13},{10,... | collective-permute-start | bytes 884744 | tf_op jit(solution)/shard_map/ppermute | solution.py:52
  468.8 17.7 %collective-permute-start.77 = (bf16[192,768]{1,0:T(8,128)(2,1)}, bf16[192,768]{1,0:T(8,128)(2,1)S(1)}, u32[]{:S(2)}, u32[]{:S(2)}) collective-permute-start(bf16[192,768]{1,0:T(8,128)(2,1)} %collective-permute-done.74), channel_id=1, source_target_pairs={{0,4},{1,5},{2,6},{3,7},{4,0},{5,1},{6,2},{7,3},{8,12},{9,13},{10,... | collective-permute-start | bytes 884744 | tf_op jit(solution)/shard_map/ppermute | solution.py:52
  475.1 24.8 %collective-permute-start.91 = (bf16[192,768]{1,0:T(8,128)(2,1)}, bf16[192,768]{1,0:T(8,128)(2,1)S(1)}, u32[]{:S(2)}, u32[]{:S(2)}) collective-permute-start(bf16[192,768]{1,0:T(8,128)(2,1)} %collective-permute-done.86), channel_id=1, source_target_pairs={{0,4},{1,5},{2,6},{3,7},{4,0},{5,1},{6,2},{7,3},{8,12},{9,13},{10,... | collective-permute-start | bytes 884744 | tf_op jit(solution)/shard_map/ppermute | solution.py:52
  (149 other events, 1473.5 us)
